TPU v7x, 32 devices: a whole 2x2x4 slice. The times are simulated.
32 devices in a mesh: expert: 16 (over z, y, core), tensor: 2 (over x).
Axes of the slice: x: 2, y: 2, z: 4, core: 2. Of those that a mesh axis runs over, the one named last changes fastest.
Arguments:
- tokens: bfloat16 [128, 2048], P('expert', 'tensor'), may hold values from -6 to 6
- out_grad: bfloat16 [128, 2048], P('expert', 'tensor'), may hold values from -1.25 to 1.25
- expert_ids: int32 [128, 8], P('expert'), may hold values from 0 to 15, all different within a row; in each aligned block of 8 rows (0 to 7, 8 to 15, ...) at most 8 rows name the same one
- gate_probs: float32 [128, 8], P('expert'), may hold values from 0.05 to 0.45
- w_gate: bfloat16 [16, 2048, 1536], P('expert', None, 'tensor'), may hold values from -0.125 to 0.125
- w_up: bfloat16 [16, 2048, 1536], P('expert', None, 'tensor'), may hold values from -0.125 to 0.125
- w_down: bfloat16 [16, 1536, 2048], P('expert', 'tensor'), may hold values from -0.15625 to 0.15625
Outputs:
- mixed: bfloat16 [128, 2048], P('expert', 'tensor')
- token_grad: bfloat16 [128, 2048], P('expert', 'tensor')
- prob_grad: float32 [128, 8], P('expert')
Inputs may be any that keep to these rules, and one draw needn't show every extreme that they name: `expert_ids`: each row names 8 different experts. Within the rows of one index of expert (aligned blocks of 8 rows) no expert is named more than 8 times, a bound that some block reaches.
All inputs are finite; a program needn't handle non-finite values.
Results may differ from a plain program's by a relative error of at most 0.02.
Values may be sent and summed in bfloat16 or wider, within the bound.
A program may use at most 64 MiB of HBM per device.

v0:
```python
import jax
import jax.numpy as jnp
from jax import lax
from jax.sharding import PartitionSpec as P

TOP = 8


def capacity_of(group_rows, expert_count):
    return max(2, min(group_rows, 3 * group_rows * TOP // expert_count))


def slot_index(group_ids, expert_count, capacity):
    flat_ids = group_ids.reshape(-1)
    onehot = (flat_ids[:, None] == jnp.arange(expert_count, dtype=jnp.int32)[None, :]).astype(
        jnp.int32
    )
    before = jnp.cumsum(onehot, axis=0) - onehot
    slot_rank = jnp.sum(before * onehot, axis=1)
    return flat_ids * capacity + slot_rank


def contract_last(left, right):
    return lax.dot_general(
        left, right, (((1,), (1,)), ((), ())), preferred_element_type=jnp.float32
    )


def per_device(tokens, out_grad, expert_ids, gate_probs, w_gate, w_up, w_down):
    expert_count = lax.axis_size("expert")
    group_rows = expert_ids.shape[0]
    capacity = capacity_of(group_rows, expert_count)
    slot_total = expert_count * capacity
    slot_ids = slot_index(expert_ids, expert_count, capacity)
    slot_hits = (jnp.arange(slot_total, dtype=jnp.int32)[:, None] == slot_ids[None, :]).astype(
        jnp.float32
    )
    slot_hits = slot_hits.reshape(slot_total, group_rows, TOP)
    route_map = jnp.sum(slot_hits, axis=2).astype(jnp.bfloat16)
    weighted = jnp.sum(slot_hits * gate_probs[None, :, :], axis=2)
    gate_w = w_gate[0]
    up_w = w_up[0]
    down_w = w_down[0]
    full_tokens, full_grads = (
        lax.all_gather(tokens, "tensor", axis=1, tiled=True),
        lax.all_gather(out_grad, "tensor", axis=1, tiled=True),
    )
    send_tokens = jnp.dot(route_map, full_tokens, preferred_element_type=jnp.float32).astype(
        jnp.bfloat16
    )
    send_grads = jnp.dot(
        weighted, full_grads.astype(jnp.float32), precision=lax.Precision.HIGHEST
    ).astype(jnp.bfloat16)
    recv_tokens, recv_grads = (
        lax.all_to_all(
            send_tokens.reshape(expert_count, capacity, -1),
            "expert",
            split_axis=0,
            concat_axis=0,
            tiled=True,
        ),
        lax.all_to_all(
            send_grads.reshape(expert_count, capacity, -1),
            "expert",
            split_axis=0,
            concat_axis=0,
            tiled=True,
        ),
    )
    recv_tokens = recv_tokens.reshape(slot_total, -1)
    recv_grads = recv_grads.reshape(slot_total, -1)
    gate_pre = jnp.dot(recv_tokens, gate_w, preferred_element_type=jnp.float32)
    up_pre = jnp.dot(recv_tokens, up_w, preferred_element_type=jnp.float32)
    hidden_grad = contract_last(recv_grads, down_w)
    gate_sig = jax.nn.sigmoid(gate_pre)
    hidden = (gate_pre * gate_sig * up_pre).astype(jnp.bfloat16)
    part_out = jnp.dot(hidden, down_w, preferred_element_type=jnp.float32)
    grad_gate = (hidden_grad * up_pre * gate_sig * (1.0 + gate_pre * (1.0 - gate_sig))).astype(
        jnp.bfloat16
    )
    grad_up = (hidden_grad * gate_pre * gate_sig).astype(jnp.bfloat16)
    part_back = contract_last(grad_gate, gate_w) + contract_last(grad_up, up_w)
    sum_out, sum_back = (
        lax.psum_scatter(
            part_out.astype(jnp.bfloat16), "tensor", scatter_dimension=1, tiled=True
        ).astype(jnp.float32),
        lax.psum_scatter(
            part_back.astype(jnp.bfloat16), "tensor", scatter_dimension=1, tiled=True
        ).astype(jnp.float32),
    )
    back_out, back_grad = (
        lax.all_to_all(
            sum_out.astype(jnp.bfloat16).reshape(expert_count, capacity, -1),
            "expert",
            split_axis=0,
            concat_axis=0,
            tiled=True,
        ),
        lax.all_to_all(
            sum_back.astype(jnp.bfloat16).reshape(expert_count, capacity, -1),
            "expert",
            split_axis=0,
            concat_axis=0,
            tiled=True,
        ),
    )
    expert_out = back_out.reshape(slot_total, -1)
    expert_back = back_grad.reshape(slot_total, -1)
    token_out = jnp.take(expert_out, slot_ids, axis=0).reshape(group_rows, TOP, -1)
    token_back = jnp.take(expert_back, slot_ids, axis=0).reshape(group_rows, TOP, -1)
    mixed = jnp.einsum(
        "gk,gkc->gc", gate_probs, token_out.astype(jnp.float32), precision=lax.Precision.HIGHEST
    ).astype(jnp.bfloat16)
    partial_inner = jnp.einsum(
        "gc,gkc->gk", out_grad, token_out, preferred_element_type=jnp.float32
    )
    prob_grad = lax.psum(partial_inner, "tensor")
    token_grad = jnp.sum(token_back.astype(jnp.float32), axis=1).astype(jnp.bfloat16)
    return (mixed, token_grad, prob_grad)


def solution(mesh):
    placed = (
        P("expert", "tensor"),
        P("expert", "tensor"),
        P("expert", None),
        P("expert", None),
        P("expert", None, "tensor"),
        P("expert", None, "tensor"),
        P("expert", "tensor", None),
    )
    return jax.shard_map(
        per_device,
        mesh=mesh,
        in_specs=placed,
        out_specs=(P("expert", "tensor"), P("expert", "tensor"), P("expert", None)),
        check_vma=False,
    )
```

profile of v0, /device:TPU:0, one launch (start us, length us, event | category | flops | bytes accessed | tf_op | source)
XLA Modules:
  0.0 130.4 jit_solution(5491228126065003342)
XLA Ops:
  7.2 0.0 copy-start
  7.2 0.9 eq.30
  8.1 0.0 copy-start.4
  8.1 0.1 fusion.34
  8.2 0.1 reduce_window_sum.11
  8.3 0.2 select_reduce_fusion.1
  8.5 0.0 copy-start.5
  8.5 0.1 reduce_sum.42
  8.5 0.7 multiply_add_fusion
  9.2 5.6 %all_gather.6 = bf16[8,2048]{1,0:T(8,128)(2,1)S(1)} all-gather(bf16[8,1024]{1,0:T(8,128)(2,1)} %param.9), channel_id=1, replica_groups=mesh['expert'=16,'tensor'=2] {'tensor'}, dimensions={1}, use_global_device_ids=true | all-gather | bytes 49152 | tf_op jit(solution)/shard_map/all_gather | solution.py:45
  14.8 0.8 select_reduce_fusion
  15.6 1.1 fusion.22
  16.7 6.5 %all-to-all-start = ((bf16[16,8,2048]{2,1,0:T(8,128)(2,1)}), bf16[16,8,2048]{2,1,0:T(8,128)(2,1)}, u32[]{:S(2)}, u32[]{:S(2)}) async-start(bf16[16,8,2048]{2,1,0:T(8,128)(2,1)} %fusion.22), calls=%async_computation | async-start | bytes 1048576 | tf_op jit(solution)/shard_map/all_to_all | solution.py:55
  23.2 4.6 %all_gather.7 = bf16[8,2048]{1,0:T(8,128)(2,1)S(1)} all-gather(bf16[8,1024]{1,0:T(8,128)(2,1)} %param.10), channel_id=1, replica_groups=mesh['expert'=16,'tensor'=2] {'tensor'}, dimensions={1}, use_global_device_ids=true | all-gather | bytes 49152 | tf_op jit(solution)/shard_map/all_gather | solution.py:46
  27.9 1.4 %fusion.21 = bf16[16,8,2048]{2,1,0:T(8,128)(2,1)} fusion(f32[128,8]{0,1:T(8,128)S(1)} %get-tuple-element.4, bf16[8,2048]{1,0:T(8,128)(2,1)S(1)} %all_gather.7), kind=kOutput, calls=%fused_computation.19 | convolution fusion | flops 25427968 | bytes 561152 | tf_op jit(solution)/shard_map/dot_general | solution.py:51
  29.3 8.5 %all-to-all-done = bf16[16,8,2048]{2,1,0:T(8,128)(2,1)} async-done(((bf16[16,8,2048]{2,1,0:T(8,128)(2,1)}), bf16[16,8,2048]{2,1,0:T(8,128)(2,1)}, u32[]{:S(2)}, u32[]{:S(2)}) %all-to-all-start) | async-done | bytes 524320 | tf_op jit(solution)/shard_map/all_to_all | solution.py:55
  37.8 4.2 %all-to-all-start.2 = ((bf16[16,8,2048]{2,1,0:T(8,128)(2,1)}), bf16[16,8,2048]{2,1,0:T(8,128)(2,1)}, u32[]{:S(2)}, u32[]{:S(2)}) async-start(bf16[16,8,2048]{2,1,0:T(8,128)(2,1)} %fusion.21), calls=%async_computation.3 | async-start | bytes 1048576 | tf_op jit(solution)/shard_map/all_to_all | solution.py:62
  42.0 0.0 copy-done.4
  42.0 0.0 copy-done.5
  42.0 0.0 reduce-scatter.5.cloned.1.call-start
  42.1 2.6 %fusion.10 = f32[128,768]{1,0:T(8,128)S(1)} fusion(bf16[1,2048,768]{2,1,0:T(8,128)(2,1)} %param.13, bf16[16,8,2048]{2,1,0:T(8,128)(2,1)} %all-to-all-done), kind=kOutput, calls=%fused_computation.12 | convolution fusion | flops 402653184 | bytes 4063232 | tf_op jit(solution)/shard_map/dot_general | solution.py:72
  44.7 11.7 %all-to-all-done.2 = bf16[16,8,2048]{2,1,0:T(8,128)(2,1)} async-done(((bf16[16,8,2048]{2,1,0:T(8,128)(2,1)}), bf16[16,8,2048]{2,1,0:T(8,128)(2,1)}, u32[]{:S(2)}, u32[]{:S(2)}) %all-to-all-start.2) | async-done | bytes 524320 | tf_op jit(solution)/shard_map/all_to_all | solution.py:62
  56.5 3.2 %fusion = f32[128,768]{1,0:T(8,128)S(1)} fusion(bf16[1,768,2048]{2,1,0:T(8,128)(2,1)} %param.15, bf16[16,8,2048]{2,1,0:T(8,128)(2,1)} %all-to-all-done.2), kind=kOutput, calls=%fused_computation.2 | convolution fusion | flops 402653184 | bytes 4063232 | tf_op jit(solution)/shard_map/dot_general | solution.py:24
  59.7 0.0 copy-done
  59.7 1.1 fusion.4
  60.9 0.0 copy-start.1
  60.9 1.8 %fusion.6 = f32[128,768]{1,0:T(8,128)S(1)} fusion(bf16[1,2048,768]{2,1,0:T(8,128)(2,1)S(1)} %copy-done, bf16[16,8,2048]{2,1,0:T(8,128)(2,1)} %all-to-all-done), kind=kOutput, calls=%fused_computation.8 | convolution fusion | flops 402653184 | bytes 4063232 | tf_op jit(solution)/shard_map/dot_general | solution.py:73
  62.7 0.0 copy-start.2
  62.7 0.7 copy-done.2
  63.4 0.0 copy-done.1
  63.4 1.9 %fusion.15 = bf16[128,2048]{1,0:T(8,128)(2,1)} fusion(f32[128,2048]{1,0:T(8,128)S(1)} %fusion.4, bf16[1,2048,768]{2,1,0:T(8,128)(2,1)S(1)} %copy-done.1, f32[128,768]{1,0:T(8,128)S(1)} %fusion.10, f32[128,768]{1,0:T(8,128)S(1)} %fusion, f32[128,768]{1,0:T(8,128)S(1)} %fusion.6), kind=kOutput, calls=%fused_computation.15 | convolution fusion | flops 404160512 | bytes 5898240 | tf_op jit(solution)/shard_map/dot_general | solution.py:24
  65.4 0.0 reduce-scatter.5.cloned.1.call-update
  65.4 0.0 reduce-scatter.3.cloned.1.call-start
  65.4 3.4 %fusion.18 = bf16[128,2048]{1,0:T(8,128)(2,1)} fusion(bf16[1,768,2048]{2,1,0:T(8,128)(2,1)} %param.15, f32[128,768]{1,0:T(8,128)} %copy-done.2, f32[128,768]{1,0:T(8,128)S(1)} %fusion.10), kind=kOutput, calls=%fused_computation.16 | convolution fusion | flops 403505152 | bytes 4456448 | tf_op jit(solution)/shard_map/dot_general | solution.py:77
  68.9 0.0 copy-start.3
  68.9 0.0 reduce-scatter.3.cloned.1.call-update
  68.9 10.5 %reduce-scatter.5.cloned.1.call-done = bf16[128,1024]{1,0:T(8,128)(2,1)} async-done(((bf16[128,2048]{1,0:T(8,128)(2,1)}), bf16[128,1024]{1,0:T(8,128)(2,1)}) %reduce-scatter.5.cloned.1.call-update) | async-done | bytes 262160 | tf_op jit(solution)/shard_map/reduce_scatter | solution.py:87
  79.4 5.6 %all-to-all-start.3 = ((bf16[16,8,1024]{2,1,0:T(8,128)(2,1)}), bf16[16,8,1024]{2,1,0:T(8,128)(2,1)S(1)}, u32[]{:S(2)}, u32[]{:S(2)}) async-start(bf16[16,8,1024]{2,1,0:T(8,128)(2,1)} %bitcast.60), calls=%async_computation.5 | async-start | bytes 524288 | tf_op jit(solution)/shard_map/all_to_all | solution.py:99
  85.1 11.3 %reduce-scatter.3.cloned.1.call-done = bf16[128,1024]{1,0:T(8,128)(2,1)} async-done(((bf16[128,2048]{1,0:T(8,128)(2,1)}), bf16[128,1024]{1,0:T(8,128)(2,1)}) %reduce-scatter.3.cloned.1.call-update) | async-done | bytes 262160 | tf_op jit(solution)/shard_map/reduce_scatter | solution.py:84
  96.4 0.0 all-to-all-done.3
  96.4 5.7 %all-to-all-start.1 = ((bf16[16,8,1024]{2,1,0:T(8,128)(2,1)}), bf16[16,8,1024]{2,1,0:T(8,128)(2,1)}, u32[]{:S(2)}, u32[]{:S(2)}) async-start(bf16[16,8,1024]{2,1,0:T(8,128)(2,1)} %bitcast.59), calls=%async_computation.2 | async-start | bytes 524288 | tf_op jit(solution)/shard_map/all_to_all | solution.py:92
  102.0 1.2 compare_and_fusion
  103.2 0.6 pad_clamp_fusion
  103.8 0.8 gather_fusion.1
  104.7 7.5 %all-to-all-done.1 = bf16[16,8,1024]{2,1,0:T(8,128)(2,1)} async-done(((bf16[16,8,1024]{2,1,0:T(8,128)(2,1)}), bf16[16,8,1024]{2,1,0:T(8,128)(2,1)}, u32[]{:S(2)}, u32[]{:S(2)}) %all-to-all-start.1) | async-done | bytes 262176 | tf_op jit(solution)/shard_map/all_to_all | solution.py:92
  112.2 1.9 %gather_fusion = bf16[64,1024]{1,0:T(8,128)(2,1)S(1)} fusion(bf16[128,1024]{1,0:T(8,128)(2,1)} %bitcast.6, s32[1024]{0:T(1024)} %pad_clamp_fusion), kind=kCustom, calls=%fused_computation.clone | custom fusion | bytes 262400 | tf_op jit(solution)/shard_map/jit(_take)/gather | solution.py:109
  114.1 1.4 %bitcast_reduce_fusion = bf16[8,1024]{1,0:T(8,128)(2,1)} fusion(bf16[64,1024]{1,0:T(8,128)(2,1)S(1)} %gather_fusion.1, pred[64]{0:T(512)(128)(4,1)} %get-tuple-element.6), kind=kLoop, calls=%fused_computation.31 | loop fusion | flops 122880 | bytes 147520 | tf_op jit(solution)/shard_map/reduce_sum | solution.py:118
  115.4 0.0 copy-done.3
  115.5 0.9 fusion.29
  116.4 5.5 %psum.7 = f32[8,8]{1,0:T(8,128)} all-reduce(f32[8,8]{1,0:T(8,128)S(1)} %bitcast.64), channel_id=1, replica_groups=mesh['expert'=16,'tensor'=2] {'tensor'}, use_global_device_ids=true, to_apply=%region_7.9 | all-reduce | flops 64 | bytes 512 | tf_op jit(solution)/shard_map/psum | solution.py:117
  121.9 1.0 fusion.31
  122.9 0.6 copy.17
Async XLA Ops:
  7.2 52.5 %copy-start = (bf16[1,2048,768]{2,1,0:T(8,128)(2,1)S(1)}, bf16[1,2048,768]{2,1,0:T(8,128)(2,1)}, u32[]{:S(2)}) copy-start(bf16[1,2048,768]{2,1,0:T(8,128)(2,1)} %param.14) | copy-start | bytes 9437188
  8.1 33.9 %copy-start.4 = (s32[64]{0:T(128)}, s32[64]{0:T(128)S(1)}, u32[]{:S(2)}) copy-start(s32[64]{0:T(128)S(1)} %eq.30) | copy-start | bytes 772
  8.5 33.6 %copy-start.5 = (s32[64]{0:T(128)}, s32[64]{0:T(128)S(1)}, u32[]{:S(2)}) copy-start(s32[64]{0:T(128)S(1)} %select_reduce_fusion.1) | copy-start | bytes 772
  16.7 21.0 %all-to-all-start = ((bf16[16,8,2048]{2,1,0:T(8,128)(2,1)}), bf16[16,8,2048]{2,1,0:T(8,128)(2,1)}, u32[]{:S(2)}, u32[]{:S(2)}) async-start(bf16[16,8,2048]{2,1,0:T(8,128)(2,1)} %fusion.22), calls=%async_computation | async-start | bytes 1048576 | tf_op jit(solution)/shard_map/all_to_all | solution.py:55
  37.8 18.7 %all-to-all-start.2 = ((bf16[16,8,2048]{2,1,0:T(8,128)(2,1)}), bf16[16,8,2048]{2,1,0:T(8,128)(2,1)}, u32[]{:S(2)}, u32[]{:S(2)}) async-start(bf16[16,8,2048]{2,1,0:T(8,128)(2,1)} %fusion.21), calls=%async_computation.3 | async-start | bytes 1048576 | tf_op jit(solution)/shard_map/all_to_all | solution.py:62
  42.0 37.4 %reduce-scatter.5.cloned.1.call-start = ((), (), s32[]{:S(2)}) async-start(), calls=%async_computation.7 | async-start | bytes 786432 | tf_op jit(solution)/shard_map/reduce_scatter | solution.py:87
  60.9 2.5 %copy-start.1 = (bf16[1,2048,768]{2,1,0:T(8,128)(2,1)S(1)}, bf16[1,2048,768]{2,1,0:T(8,128)(2,1)}, u32[]{:S(2)}) copy-start(bf16[1,2048,768]{2,1,0:T(8,128)(2,1)} %param.13) | copy-start | bytes 9437188
  62.7 0.7 copy-start.2
  65.4 31.0 %reduce-scatter.3.cloned.1.call-start = ((), (), s32[]{:S(2)}) async-start(), calls=%async_computation.6 | async-start | bytes 786432 | tf_op jit(solution)/shard_map/reduce_scatter | solution.py:84
  68.9 46.6 %copy-start.3 = (bf16[8,1024]{1,0:T(8,128)(2,1)S(1)}, bf16[8,1024]{1,0:T(8,128)(2,1)}, u32[]{:S(2)}) copy-start(bf16[8,1024]{1,0:T(8,128)(2,1)} %param.10) | copy-start | bytes 49156
  79.4 16.9 %all-to-all-start.3 = ((bf16[16,8,1024]{2,1,0:T(8,128)(2,1)}), bf16[16,8,1024]{2,1,0:T(8,128)(2,1)S(1)}, u32[]{:S(2)}, u32[]{:S(2)}) async-start(bf16[16,8,1024]{2,1,0:T(8,128)(2,1)} %bitcast.60), calls=%async_computation.5 | async-start | bytes 524288 | tf_op jit(solution)/shard_map/all_to_all | solution.py:99
  96.4 15.8 %all-to-all-start.1 = ((bf16[16,8,1024]{2,1,0:T(8,128)(2,1)}), bf16[16,8,1024]{2,1,0:T(8,128)(2,1)}, u32[]{:S(2)}, u32[]{:S(2)}) async-start(bf16[16,8,1024]{2,1,0:T(8,128)(2,1)} %bitcast.59), calls=%async_computation.2 | async-start | bytes 524288 | tf_op jit(solution)/shard_map/all_to_all | solution.py:92
Sparse Core Ops, SparseCore 0:
  65.5 13.8 reduce-scatter.4
  81.8 14.5 reduce-scatter.2
where the time goes:
time: 131 us; the launch traced here: 130 us
  waiting for transfers between devices  49.6 us (38%)
  starting transfers between devices  22.1 us (17%)
  matrix products  18.7 us (14%)
  blocking collectives  15.7 us (12%)
  between operations  14.2 us (11%)
  local copies, waits for them, and re-layouts  5.1 us (4%)
  other arithmetic  5 us (4%)
    all_to_all x1, waiting for transfers between devices, per_device(): lax.all_to_all(send_grads.reshape(expert_count, capacity, -1), 'expert',...  11.7 us
    reduce_scatter x1, waiting for transfers between devices, per_device(): lax.psum_scatter(part_out.astype(jnp.bfloat16), 'tensor', scatter_dimensi...  11.3 us
    reduce_scatter x1, waiting for transfers between devices, per_device(): lax.psum_scatter(part_back.astype(jnp.bfloat16), 'tensor', scatter_dimens...  10.5 us
    all_to_all x1, waiting for transfers between devices, per_device(): lax.all_to_all(send_tokens.reshape(expert_count, capacity, -1), 'expert',...  8.46 us
    all_to_all x1, waiting for transfers between devices, per_device(): lax.all_to_all(sum_out.astype(jnp.bfloat16).reshape(expert_count, capacit...  7.48 us
    all_to_all x1, starting transfers between devices, per_device(): lax.all_to_all(send_tokens.reshape(expert_count, capacity, -1), 'expert',...  6.48 us
    dot_general x3, matrix products, contract_last(): lax.dot_general(left, right, (((1,), (1,)), ((), ())), preferred_element_...  6.33 us
    all_to_all x1, starting transfers between devices, per_device(): lax.all_to_all(sum_out.astype(jnp.bfloat16).reshape(expert_count, capacit...  5.65 us
  transfers between devices with their start and end apart: 6, of which 5 were waited for; matrix products, arithmetic and copies ran while one was open for 8% of the time, Pallas kernels for 0%

commit v1 on v0

v1 whole, which is shorter than its diff:
```python
import functools

import jax
import jax.numpy as jnp
from jax import lax
from jax.experimental import pallas as pl
from jax.experimental.pallas import tpu as pltpu
from jax.sharding import PartitionSpec as P

CORES = 2
LANES = 128
MESH = pl.DeviceIdType.MESH


def grid_of(expert_count):
    chips = expert_count // CORES
    fast = 1
    while (fast * 2) * (fast * 2) <= chips:
        fast *= 2
    return chips // fast, fast


def dot_nn(left, right):
    return jnp.dot(left, right, preferred_element_type=jnp.float32)


def dot_nt(left, right):
    return lax.dot_general(
        left, right, (((1,), (1,)), ((), ())), preferred_element_type=jnp.float32
    )


def kernel(
    A, B, T, count,
    tok_ref, grad_ref, ids_ref, prob_ref, wg_hbm, wu_hbm, wd_hbm,
    mixed_ref, tgrad_ref, pgrad_ref,
    wg, wu, wd, g0, g1, pg, xs, og, hid, gga, gup,
    r0, r1, rc0, rc1, s0, s1, rx0, ry1, u0, u1, ry0, rx1, v0, v1, rz0, rz1,
    qr, qc, qx, qt, qy, qv, qz,
    wsem, ssem, rsem,
):
    me = lax.axis_index("expert")
    t = lax.axis_index("tensor")
    c = lax.rem(me, CORES)
    b = lax.rem(lax.div(me, CORES), B)
    a = lax.div(me, CORES * B)
    group, feats = tok_ref.shape
    half = feats // 2
    lanes = pg.shape[-1]
    rows = xs.shape[0]

    def spot(aa, bb, cc, tt):
        return ((aa * B + bb) * CORES + cc, tt)

    def turn(value, r, size):
        return lax.rem(value + r, size)

    to_a = [spot(turn(a, r, A), b, c, t) for r in range(1, A)]
    to_b = [spot(a, turn(b, r, B), c, t) for r in range(1, B)]
    to_t = [spot(a, b, c, turn(t, r, T)) for r in range(1, T)]
    to_c = spot(a, b, 1 - c, t)

    loads = [
        pltpu.make_async_copy(src.at[0], dst, wsem.at[i])
        for i, (src, dst) in enumerate(((wg_hbm, wg), (wu_hbm, wu), (wd_hbm, wd)))
    ]
    for load in loads:
        load.start()

    barrier = pltpu.get_barrier_semaphore()
    peers = to_a + to_b + to_t + [to_c]
    for peer in peers:
        pl.semaphore_signal(barrier, inc=1, device_id=peer, device_id_type=MESH)

    ids = ids_ref[...]
    probs = prob_ref[...]
    lane = lax.broadcasted_iota(jnp.int32, (group, lanes), 1)
    routed = jnp.zeros((group, lanes), jnp.float32)
    for k in range(ids.shape[1]):
        routed = routed + jnp.where(lane == ids[:, k : k + 1], probs[:, k : k + 1], 0.0)
    unit = jnp.concatenate(
        [tok_ref[...].astype(jnp.float32), grad_ref[...].astype(jnp.float32)], axis=0
    ).astype(jnp.bfloat16)
    g0[c, t, b, a] = unit[:, :half]
    g1[c, b, t, a] = unit[:, half:]
    pg[c, b, a] = routed
    pl.semaphore_wait(barrier, len(peers))

    started = []

    def send(src, dst, peer):
        i = len(started)
        copy = pltpu.make_async_remote_copy(
            src_ref=src, dst_ref=dst, send_sem=ssem.at[i], recv_sem=rsem.at[i],
            device_id=peer, device_id_type=MESH,
        )
        copy.start()
        started.append(copy)
        return copy

    def same(ref, peers):
        return [send(ref, ref, peer) for peer in peers]

    def arrive(copies):
        for copy in copies:
            copy.wait_recv()

    a0 = same(g0.at[c, t, b, a], to_a)
    a1 = same(g1.at[c, b, t, a], to_a)
    ap = same(pg.at[c, b, a], to_a)
    arrive(a0)
    b0 = same(g0.at[c, t, b], to_b)
    arrive(a1)
    b1 = same(g1.at[c, b, t], to_t)
    arrive(ap)
    bp = same(pg.at[c, b], to_b)
    arrive(b0)
    c0 = same(g0.at[c, t], to_t)
    arrive(b1)
    c1 = same(g1.at[c, b], to_b)
    arrive(bp)
    dp = same(pg.at[c], [to_c])
    arrive(c0)
    d0 = same(g0.at[c], [to_c])
    arrive(c1)
    d1 = same(g1.at[c], [to_c])
    arrive(dp)
    arrive(d0)
    arrive(d1)

    part = B * A * group
    for cc in range(CORES):
        for tt in range(T):
            for h in range(2):
                block = g0[cc, tt] if h == 0 else g1[cc, :, tt]
                block = block.astype(jnp.float32)
                at = (pl.ds(cc * part, part), pl.ds(tt * feats + h * half, half))
                xs[at] = block[:, :, :group].reshape(part, half).astype(jnp.bfloat16)
                og[at] = block[:, :, group:].reshape(part, half).astype(jnp.bfloat16)

    for load in loads:
        load.wait()

    step = min(rows, 256)
    tiles = step // group

    def first(i):
        at = pl.ds(i * step if isinstance(i, int) else pl.multiple_of(i * step, step), step)
        weights = pg.reshape(rows, lanes)[at, :]
        mine = lax.broadcasted_iota(jnp.int32, (step, lanes), 1) == me
        weight = jnp.sum(jnp.where(mine, weights, 0.0), axis=1, keepdims=True)
        gate = dot_nn(xs[at, :], wg[...])
        up = dot_nn(xs[at, :], wu[...])
        back = dot_nt(og[at, :], wd[...])
        sig = jax.nn.sigmoid(gate)
        silu = gate * sig
        hidden = silu * up
        inner = jnp.sum(hidden * back, axis=1, keepdims=True)
        back = back * weight
        hid[at, :] = (hidden * weight).astype(jnp.bfloat16)
        gga[at, :] = (back * up * sig * (1.0 + gate * (1.0 - sig))).astype(jnp.bfloat16)
        gup[at, :] = (back * silu).astype(jnp.bfloat16)
        qr.reshape(rows, lanes)[at, :] = jnp.where(mine, inner, 0.0)

    if rows == step:
        first(0)
    else:
        pl.loop(0, rows // step)(first)

    ec = send(qr.at[1 - c], qc, to_c)

    cuts = CORES if rows > 256 else 1

    def second(h, r):
        tt = turn(t, r, T)
        ref, landing = ((r0, rc0), (r1, rc1))[h]
        cols = pl.ds(pl.multiple_of(tt * feats + h * half, half), half)
        size = rows // cuts
        for i in range(cuts):
            at = pl.ds(i * size, size)
            out = dot_nn(hid[at, :], wd[:, cols])
            back = dot_nt(gga[at, :], wg[cols, :]) + dot_nt(gup[at, :], wu[cols, :])
            shape = (CORES // cuts, B, A, group, half)
            block = jnp.concatenate([out.reshape(shape), back.reshape(shape)], axis=3)
            block = block.astype(jnp.bfloat16)
            for j in range(CORES // cuts):
                ref[i + j, tt] = block[j]
        return send(ref.at[1 - c, tt], landing.at[tt], to_c)

    def wide(value):
        return value.astype(jnp.float32)

    def narrow(value):
        return value.astype(jnp.bfloat16)

    def total(first_term, ref):
        value = wide(first_term)
        for i in range(ref.shape[0]):
            value = value + wide(ref[i])
        return value

    e0 = [second(0, r) for r in list(range(1, T)) + [0]]
    f0 = []
    for r in range(1, T):
        e0[r - 1].wait_recv()
        tt = turn(t, r, T)
        s0[tt] = narrow(wide(r0[c, tt]) + wide(rc0[tt]))
        f0.append(send(s0.at[tt], rx0.at[r - 1], to_t[r - 1]))
    e1 = [second(1, r) for r in list(range(1, T)) + [0]]
    ec.wait_recv()
    qx[t] = qr[c] + qc[...]
    fq = same(qx.at[t], to_t)
    e0[T - 1].wait_recv()
    s0[t] = narrow(wide(r0[c, t]) + wide(rc0[t]))
    arrive(e1)
    f1 = []
    for r in list(range(1, B)) + [0]:
        bb = turn(b, r, B)
        s1[bb] = narrow(wide(r1[c, :, bb]) + wide(rc1[:, bb]))
        if r:
            f1.append(send(s1.at[bb], ry1.at[r - 1], to_b[r - 1]))
    arrive(f0)
    u0[...] = narrow(total(s0[t], rx0))
    h0 = [send(u0.at[turn(b, r, B)], ry0.at[r - 1], to_b[r - 1]) for r in range(1, B)]
    arrive(fq)
    value = qx[0]
    for i in range(1, T):
        value = value + qx[i]
    qt[...] = value
    hq = [send(qt.at[turn(b, r, B)], qy.at[r - 1], to_b[r - 1]) for r in range(1, B)]
    arrive(f1)
    u1[...] = narrow(total(s1[b], ry1))
    h1 = [send(u1.at[turn(t, r, T)], rx1.at[r - 1], to_t[r - 1]) for r in range(1, T)]
    arrive(h0)
    v0[...] = narrow(total(u0[b], ry0))
    k0 = [send(v0.at[turn(a, r, A)], rz0.at[r - 1], to_a[r - 1]) for r in range(1, A)]
    arrive(hq)
    qv[...] = total(qt[b], qy)
    kq = [send(qv.at[turn(a, r, A)], qz.at[r - 1], to_a[r - 1]) for r in range(1, A)]
    arrive(h1)
    v1[...] = narrow(total(u1[t], rx1))
    k1 = [send(v1.at[turn(a, r, A)], rz1.at[r - 1], to_a[r - 1]) for r in range(1, A)]
    arrive(k0)
    last = total(v0[a], rz0)
    mixed_ref[:, :half] = narrow(last[:group])
    tgrad_ref[:, :half] = narrow(last[group:])
    arrive(kq)
    inner = total(qv[a], qz)
    column = lax.broadcasted_iota(jnp.int32, ids.shape, 1)
    result = jnp.zeros(ids.shape, jnp.float32)
    for k in range(ids.shape[1]):
        one = jnp.sum(jnp.where(lane == ids[:, k : k + 1], inner, 0.0), axis=1, keepdims=True)
        result = jnp.where(column == k, one, result)
    pgrad_ref[...] = result
    arrive(k1)
    last = total(v1[a], rz1)
    mixed_ref[:, half:] = narrow(last[:group])
    tgrad_ref[:, half:] = narrow(last[group:])
    assert len(started) == count
    for copy in started:
        copy.wait_send()


def per_device(tokens, out_grad, expert_ids, gate_probs, w_gate, w_up, w_down):
    E = lax.axis_size("expert")
    T = lax.axis_size("tensor")
    A, B = grid_of(E)
    C = CORES
    group, feats = tokens.shape
    width = feats * T
    hidden = w_gate.shape[2]
    half = feats // 2
    rows = E * group
    lanes = -(-E // LANES) * LANES
    bf, f32 = jnp.bfloat16, jnp.float32
    pair = (2 * group, half)
    tile = (group, lanes)
    na, nb, nt = A - 1, B - 1, T - 1
    count = 3 * na + 2 * nb + nt + nt + nb + 3 + 1 + 2 * T + 2 * nt + nb + 2 * nb + nt + 3 * na

    def vm(*shape, dtype=bf):
        return pltpu.VMEM(shape, dtype)

    scratch = [
        vm(width, hidden), vm(width, hidden), vm(hidden, width),
        vm(C, T, B, A, *pair), vm(C, B, T, A, *pair), vm(C, B, A, *tile, dtype=f32),
        vm(rows, width), vm(rows, width),
        vm(rows, hidden), vm(rows, hidden), vm(rows, hidden),
        vm(C, T, B, A, *pair), vm(C, T, B, A, *pair),
        vm(T, B, A, *pair), vm(T, B, A, *pair),
        vm(T, B, A, *pair), vm(B, T, A, *pair),
        vm(nt, B, A, *pair), vm(nb, T, A, *pair),
        vm(B, A, *pair), vm(T, A, *pair),
        vm(nb, A, *pair), vm(nt, A, *pair),
        vm(A, *pair), vm(A, *pair),
        vm(na, *pair), vm(na, *pair),
        vm(C, B, A, *tile, dtype=f32), vm(B, A, *tile, dtype=f32),
        vm(T, B, A, *tile, dtype=f32), vm(B, A, *tile, dtype=f32),
        vm(nb, A, *tile, dtype=f32), vm(A, *tile, dtype=f32),
        vm(na, *tile, dtype=f32),
        pltpu.SemaphoreType.DMA((3,)),
        pltpu.SemaphoreType.DMA((count,)),
        pltpu.SemaphoreType.DMA((count,)),
    ]
    inside = pl.BlockSpec(memory_space=pltpu.VMEM)
    outside = pl.BlockSpec(memory_space=pl.ANY)
    return pl.pallas_call(
        functools.partial(kernel, A, B, T, count),
        out_shape=(
            jax.ShapeDtypeStruct((group, feats), bf),
            jax.ShapeDtypeStruct((group, feats), bf),
            jax.ShapeDtypeStruct(expert_ids.shape, f32),
        ),
        in_specs=[inside] * 4 + [outside] * 3,
        out_specs=(inside, inside, inside),
        scratch_shapes=scratch,
        compiler_params=pltpu.CompilerParams(
            collective_id=0, has_side_effects=True, vmem_limit_bytes=58 * 1024 * 1024
        ),
        cost_estimate=pl.CostEstimate(
            flops=12 * rows * width * hidden,
            bytes_accessed=6 * width * hidden,
            transcendentals=rows * hidden,
        ),
    )(tokens, out_grad, expert_ids, gate_probs, w_gate, w_up, w_down)


def solution(mesh):
    placed = (
        P("expert", "tensor"),
        P("expert", "tensor"),
        P("expert", None),
        P("expert", None),
        P("expert", None, "tensor"),
        P("expert", None, "tensor"),
        P("expert", "tensor", None),
    )
    return jax.shard_map(
        per_device,
        mesh=mesh,
        in_specs=placed,
        out_specs=(P("expert", "tensor"), P("expert", "tensor"), P("expert", None)),
        check_vma=False,
    )
```

time: 131 us -> 46.5 us (0.35)
  waiting for transfers between devices: 49.6 us -> 0 us
  Pallas kernels: 0 us -> 41.5 us
  starting transfers between devices: 22.1 us -> 0 us
  matrix products: 18.7 us -> 0 us
  blocking collectives: 15.7 us -> 0 us
  between operations: 14.2 us -> 0.64 us
  other arithmetic: 5 us -> 0 us
    pallas_call x0 -> x1, Pallas kernels: none -> 41.5 us  [per_device(): pl.pallas_call(functools.partial(kernel, A, B, T, count), out_shape=(jax....]
    all_to_all x4 -> x0, waiting for transfers between devices: 27.7 us -> none  [the longest x1 11.7 us: per_device(): lax.all_to_all(send_grads.reshape(expert_count, capacity, -1), 'expert',...]
    all_to_all x4 -> x0, starting transfers between devices: 22 us -> none  [the longest x1 6.48 us: per_device(): lax.all_to_all(send_tokens.reshape(expert_count, capacity, -1), 'expert',...]
    reduce_scatter x2 -> x0, waiting for transfers between devices: 21.9 us -> none  [the longest x1 11.3 us: per_device(): lax.psum_scatter(part_out.astype(jnp.bfloat16), 'tensor', scatter_dimensi...]
    dot_general x10 -> x0, matrix products: 18.7 us -> none  [the longest x3 6.33 us: contract_last(): lax.dot_general(left, right, (((1,), (1,)), ((), ())), preferred_element_...]
    all_gather x2 -> x0, blocking collectives: 10.2 us -> none  [the longest x1 5.57 us: per_device(): lax.all_gather(tokens, 'tensor', axis=1, tiled=True)]
    psum x1 -> x0, blocking collectives: 5.52 us -> none  [per_device(): prob_grad = lax.psum(partial_inner, 'tensor')]
    unnamed x12 -> x3, local copies, waits for them, and re-layouts: 0.77 us -> 3.92 us
  transfers between devices with their start and end apart: 6 -> 0, of which waited for: 5 -> 0; matrix products, arithmetic and copies ran while one was open for 8% -> 0% of each run, Pallas kernels for 0% -> 0%
where the time goes in v1:
time: 46.5 us; the launch traced here: 46.1 us
  Pallas kernels  41.5 us (89%)
  local copies, waits for them, and re-layouts  3.92 us (8%)
  between operations  0.64 us (1%)
    pallas_call x1, Pallas kernels, per_device(): pl.pallas_call(functools.partial(kernel, A, B, T, count), out_shape=(jax....  41.5 us
    unnamed x3, local copies, waits for them, and re-layouts  3.92 us

profile of v1, /device:TPU:0, one launch (start us, length us, event | category | flops | bytes accessed | tf_op | source)
XLA Modules:
  0.0 46.1 jit_solution(17904965698364324738)
XLA Ops:
  0.6 41.5 %shard_map.94 = (bf16[8,1024]{1,0:T(8,128)(2,1)}, bf16[8,1024]{1,0:T(8,128)(2,1)}, f32[8,8]{1,0:T(8,128)}) custom-call(bf16[8,1024]{1,0:T(8,128)(2,1)} %tok_ref.1, bf16[8,1024]{1,0:T(8,128)(2,1)} %grad_ref.1, s32[8,8]{1,0:T(8,128)} %ids_ref.1, f32[8,8]{1,0:T(8,128)} %prob_ref.1, bf16[1,2048,768]{2,1,0:T(8,128)(2,1)} %wg_hbm.1, bf16[1,2048,768]{2,1,0:T(8,128)(2,1)} %wu_hbm.1, ...), custom_call_target="tpu_custom_call" | custom-call | flops 2415919104 | bytes 9437184 | tf_op jit(solution)/shard_map/pallas_call | solution.py:307
  42.2 1.3 %copy.13 = bf16[8,1024]{1,0:T(8,128)(2,1)} copy(bf16[8,1024]{1,0:T(8,128)(2,1)} %get-tuple-element.6) | data formatting | bytes 32768
  43.5 1.3 %copy.14 = bf16[8,1024]{1,0:T(8,128)(2,1)} copy(bf16[8,1024]{1,0:T(8,128)(2,1)} %get-tuple-element.7) | data formatting | bytes 32768
  44.8 1.3 %copy.15 = f32[8,8]{1,0:T(8,128)} copy(f32[8,8]{1,0:T(8,128)} %get-tuple-element.8) | data formatting | bytes 512

commit v2 on v1

v2 whole, which is shorter than its diff:
```python
import functools

import jax
import jax.numpy as jnp
from jax import lax
from jax.experimental import pallas as pl
from jax.experimental.pallas import tpu as pltpu
from jax.sharding import PartitionSpec as P

CORES = 2
LANES = 128
PATHS = 2
PIECES = 2
MESH = pl.DeviceIdType.MESH


def grid_of(expert_count):
    chips = expert_count // CORES
    fast = 1
    while (fast * 2) * (fast * 2) <= chips:
        fast *= 2
    return chips // fast, fast


def dot_nn(left, right):
    return jnp.dot(left, right, preferred_element_type=jnp.float32)


def dot_nt(left, right):
    return lax.dot_general(
        left, right, (((1,), (1,)), ((), ())), preferred_element_type=jnp.float32
    )


def kernel(
    A, B, T, count,
    tok_ref, grad_ref, ids_ref, prob_ref, wg_hbm, wu_hbm, wd_hbm,
    mixed_ref, tgrad_ref, pgrad_ref,
    wg, wu, wd, g0, g1, pg, xs, og, hid, gga, gup, sum_gate, sum_up, sum_back,
    r0, r1, rc0, rc1, s0, s1, rx0, ry1, u0, u1, ry0, rx1, v0, v1, rz0, rz1,
    qr, qc, qx, qt, qy, qv, qz,
    wsem, ssem, rsem,
):
    me = lax.axis_index("expert")
    t = lax.axis_index("tensor")
    c = lax.rem(me, CORES)
    b = lax.rem(lax.div(me, CORES), B)
    a = lax.div(me, CORES * B)
    group, feats = tok_ref.shape
    piece = feats // (PATHS * PIECES)
    lanes = pg.shape[-1]
    rows = xs.shape[0]
    pieces = range(PIECES)

    def spot(aa, bb, cc, tt):
        return ((aa * B + bb) * CORES + cc, tt)

    def turn(value, r, size):
        return lax.rem(value + r, size)

    def column(h, s):
        return (s * PATHS + h) * piece

    to_a = [spot(turn(a, r, A), b, c, t) for r in range(1, A)]
    to_b = [spot(a, turn(b, r, B), c, t) for r in range(1, B)]
    to_t = [spot(a, b, c, turn(t, r, T)) for r in range(1, T)]
    to_c = spot(a, b, 1 - c, t)

    loads = [
        pltpu.make_async_copy(src.at[0], dst, wsem.at[i])
        for i, (src, dst) in enumerate(((wg_hbm, wg), (wu_hbm, wu), (wd_hbm, wd)))
    ]

    barrier = pltpu.get_barrier_semaphore()
    peers = to_a + to_b + to_t + [to_c]
    for peer in peers:
        pl.semaphore_signal(barrier, inc=1, device_id=peer, device_id_type=MESH)
    for load in loads:
        load.start()

    ids = ids_ref[...]
    probs = prob_ref[...]
    lane = lax.broadcasted_iota(jnp.int32, (group, lanes), 1)
    routed = jnp.zeros((group, lanes), jnp.float32)
    for k in range(ids.shape[1]):
        routed = routed + jnp.where(lane == ids[:, k : k + 1], probs[:, k : k + 1], 0.0)
    unit = jnp.concatenate(
        [tok_ref[...].astype(jnp.float32), grad_ref[...].astype(jnp.float32)], axis=0
    ).astype(jnp.bfloat16)
    for s in pieces:
        g0[s, c, t, b, a] = unit[:, column(0, s) : column(0, s) + piece]
        g1[s, c, b, t, a] = unit[:, column(1, s) : column(1, s) + piece]
    pg[c, b, a] = routed
    pl.semaphore_wait(barrier, len(peers))

    started = []

    def send(src, dst, peer):
        i = len(started)
        copy = pltpu.make_async_remote_copy(
            src_ref=src, dst_ref=dst, send_sem=ssem.at[i], recv_sem=rsem.at[i],
            device_id=peer, device_id_type=MESH,
        )
        copy.start()
        started.append(copy)
        return copy

    def same(ref, peers):
        return [send(ref, ref, peer) for peer in peers]

    def arrive(copies):
        for copy in copies:
            copy.wait_recv()

    a0, a1, b0, b1, c0, c1 = ([None] * PIECES for _ in range(6))
    for s in pieces:
        a0[s] = same(g0.at[s, c, t, b, a], to_a)
        a1[s] = same(g1.at[s, c, b, t, a], to_a)
    ap = same(pg.at[c, b, a], to_a)
    for s in pieces:
        arrive(a0[s])
        b0[s] = same(g0.at[s, c, t, b], to_b)
        arrive(a1[s])
        b1[s] = same(g1.at[s, c, b, t], to_t)
    arrive(ap)
    bp = same(pg.at[c, b], to_b)
    own, rest0, rest1 = [], [], []
    for s in pieces:
        arrive(b0[s])
        c0[s] = same(g0.at[s, c, t], to_t)
        own += same(g0.at[s, c, t], [to_c])
        arrive(b1[s])
        c1[s] = same(g1.at[s, c, b], to_b)
        rest1.append(same(g1.at[s, c, b], [to_c]))
    arrive(bp)
    dp = same(pg.at[c], [to_c])

    part = B * A * group
    step = min(rows, 256)

    def assemble(slot, h, s, r):
        tt = turn(t, r, T)
        for cc in range(CORES):
            block = g0[s, cc, tt] if h == 0 else g1[s, cc, :, tt]
            block = block.astype(jnp.float32)
            at = (pl.ds(cc * part, part), pl.ds(slot * piece, piece))
            xs[at] = block[:, :, :group].reshape(part, piece).astype(jnp.bfloat16)
            og[at] = block[:, :, group:].reshape(part, piece).astype(jnp.bfloat16)

    def products(at, runs):
        gate = up = back = None
        for slot, h, s, r, width in runs:
            start = pl.multiple_of(turn(t, r, T) * feats + column(h, s), piece)
            here = pl.ds(slot * piece, width * piece)
            there = pl.ds(start, width * piece)
            x, o = xs[at, here], og[at, here]
            terms = dot_nn(x, wg[there, :]), dot_nn(x, wu[there, :]), dot_nt(o, wd[:, there])
            if gate is None:
                gate, up, back = terms
            else:
                gate, up, back = gate + terms[0], up + terms[1], back + terms[2]
        return gate, up, back

    def by_rows(body):
        if rows == step:
            body(pl.ds(0, rows))
        else:

            @pl.loop(0, rows // step)
            def _(i):
                body(pl.ds(pl.multiple_of(i * step, step), step))

    slots = 0

    def plan(runs):
        nonlocal slots
        out = []
        for h, s, r, width in runs:
            for i in range(width):
                assemble(slots + i, h + i, s, r)
            out.append((slots, h, s, r, width))
            slots += width
        return out

    def forward0(s):
        for r in range(1, T):
            c0[s][r - 1].wait_recv()
            rest0.append(same(g0.at[s, c, turn(t, T - r, T)], [to_c]))

    def forward1(s):
        for r in range(1, B):
            c1[s][r - 1].wait_recv()
            rest1.append(same(g1.at[s, c, turn(b, B - r, B)], [to_c]))

    forward0(0)
    for load in loads:
        load.wait()
    arrive(own)
    runs = plan([(0, s, 0, 1) for s in pieces])

    def begin(at):
        sum_gate[at, :], sum_up[at, :], sum_back[at, :] = products(at, runs)

    by_rows(begin)
    for s in pieces:
        forward1(s)
        if s:
            forward0(s)
    for copies in rest0 + rest1:
        arrive(copies)
    arrive(dp)
    more = plan(
        [(0, s, r, 2) for s in pieces for r in range(1, T)] + [(1, s, 0, 1) for s in pieces]
    )

    def finish(at):
        gate, up, back = products(at, more)
        gate = gate + sum_gate[at, :]
        up = up + sum_up[at, :]
        back = back + sum_back[at, :]
        weights = pg.reshape(rows, lanes)[at, :]
        mine = lax.broadcasted_iota(jnp.int32, (step, lanes), 1) == me
        weight = jnp.sum(jnp.where(mine, weights, 0.0), axis=1, keepdims=True)
        sig = jax.nn.sigmoid(gate)
        silu = gate * sig
        hidden = silu * up
        inner = jnp.sum(hidden * back, axis=1, keepdims=True)
        back = back * weight
        hid[at, :] = (hidden * weight).astype(jnp.bfloat16)
        gga[at, :] = (back * up * sig * (1.0 + gate * (1.0 - sig))).astype(jnp.bfloat16)
        gup[at, :] = (back * silu).astype(jnp.bfloat16)
        qr.reshape(rows, lanes)[at, :] = jnp.where(mine, inner, 0.0)

    by_rows(finish)
    ec = send(qr.at[1 - c], qc, to_c)

    cuts = CORES if rows > 256 else 1

    def second(h, s, r):
        tt = turn(t, r, T)
        ref, landing = ((r0, rc0), (r1, rc1))[h]
        cols = pl.ds(pl.multiple_of(tt * feats + column(h, s), piece), piece)
        size = rows // cuts
        for i in range(cuts):
            at = pl.ds(i * size, size)
            out = dot_nn(hid[at, :], wd[:, cols])
            back = dot_nt(gga[at, :], wg[cols, :]) + dot_nt(gup[at, :], wu[cols, :])
            shape = (CORES // cuts, B, A, group, piece)
            block = jnp.concatenate([out.reshape(shape), back.reshape(shape)], axis=3)
            block = block.astype(jnp.bfloat16)
            for j in range(CORES // cuts):
                ref[s, i + j, tt] = block[j]
        return send(ref.at[s, 1 - c, tt], landing.at[s, tt], to_c)

    def wide(value):
        return value.astype(jnp.float32)

    def narrow(value):
        return value.astype(jnp.bfloat16)

    def total(first_term, ref):
        value = wide(first_term)
        for i in range(ref.shape[0]):
            value = value + wide(ref[i])
        return value

    far = list(range(1, T))
    e0 = [[None] * T for _ in pieces]
    e1 = [[None] * T for _ in pieces]
    f0, f1, h0, h1, k0, k1 = ([None] * PIECES for _ in range(6))

    def away0(s):
        f0[s] = []
        for r in far:
            e0[s][r].wait_recv()
            tt = turn(t, r, T)
            s0[s, tt] = narrow(wide(r0[s, c, tt]) + wide(rc0[s, tt]))
            f0[s].append(send(s0.at[s, tt], rx0.at[s, r - 1], to_t[r - 1]))

    def home0(s):
        e0[s][0].wait_recv()
        s0[s, t] = narrow(wide(r0[s, c, t]) + wide(rc0[s, t]))

    def away1(s):
        arrive(e1[s])
        f1[s] = []
        for r in list(range(1, B)) + [0]:
            bb = turn(b, r, B)
            s1[s, bb] = narrow(wide(r1[s, c, :, bb]) + wide(rc1[s, :, bb]))
            if r:
                f1[s].append(send(s1.at[s, bb], ry1.at[s, r - 1], to_b[r - 1]))

    def across0(s):
        arrive(f0[s])
        u0[s] = narrow(total(s0[s, t], rx0.at[s]))
        h0[s] = [
            send(u0.at[s, turn(b, r, B)], ry0.at[s, r - 1], to_b[r - 1]) for r in range(1, B)
        ]

    def across1(s):
        arrive(f1[s])
        u1[s] = narrow(total(s1[s, b], ry1.at[s]))
        h1[s] = [
            send(u1.at[s, turn(t, r, T)], rx1.at[s, r - 1], to_t[r - 1]) for r in range(1, T)
        ]

    def along0(s):
        arrive(h0[s])
        v0[s] = narrow(total(u0[s, b], ry0.at[s]))
        k0[s] = [
            send(v0.at[s, turn(a, r, A)], rz0.at[s, r - 1], to_a[r - 1]) for r in range(1, A)
        ]

    def along1(s):
        arrive(h1[s])
        v1[s] = narrow(total(u1[s, t], rx1.at[s]))
        k1[s] = [
            send(v1.at[s, turn(a, r, A)], rz1.at[s, r - 1], to_a[r - 1]) for r in range(1, A)
        ]

    for s in pieces:
        for r in far:
            e0[s][r] = second(0, s, r)
        if s:
            home0(s - 1)
        for r in far:
            e1[s][r] = second(1, s, r)
        away0(s)
        if s:
            across0(s - 1)
        else:
            ec.wait_recv()
            qx[t] = qr[c] + qc[...]
            fq = same(qx.at[t], to_t)
        e1[s][0] = second(1, s, 0)
        e0[s][0] = second(0, s, 0)
        away1(s)
    last = PIECES - 1
    for s in range(last):
        across1(s)
    home0(last)
    arrive(fq)
    value = qx[0]
    for i in range(1, T):
        value = value + qx[i]
    qt[...] = value
    hq = [send(qt.at[turn(b, r, B)], qy.at[r - 1], to_b[r - 1]) for r in range(1, B)]
    for s in range(last):
        along0(s)
    across0(last)
    arrive(hq)
    qv[...] = total(qt[b], qy)
    kq = [send(qv.at[turn(a, r, A)], qz.at[r - 1], to_a[r - 1]) for r in range(1, A)]
    for s in range(last):
        along1(s)
    across1(last)
    along0(last)

    def deliver(h, s, mine, ref, copies):
        arrive(copies)
        value = total(mine, ref)
        at = pl.ds(column(h, s), piece)
        mixed_ref[:, at] = narrow(value[:group])
        tgrad_ref[:, at] = narrow(value[group:])

    for s in range(last):
        deliver(0, s, v0[s, a], rz0.at[s], k0[s])
    arrive(kq)
    inner = total(qv[a], qz)
    place = lax.broadcasted_iota(jnp.int32, ids.shape, 1)
    result = jnp.zeros(ids.shape, jnp.float32)
    for k in range(ids.shape[1]):
        one = jnp.sum(jnp.where(lane == ids[:, k : k + 1], inner, 0.0), axis=1, keepdims=True)
        result = jnp.where(place == k, one, result)
    pgrad_ref[...] = result
    along1(last)
    for s in range(last):
        deliver(1, s, v1[s, a], rz1.at[s], k1[s])
    deliver(0, last, v0[last, a], rz0.at[last], k0[last])
    deliver(1, last, v1[last, a], rz1.at[last], k1[last])
    assert len(started) == count
    for copy in started:
        copy.wait_send()


def settle(*refs):
    for source, target in zip(refs[: len(refs) // 2], refs[len(refs) // 2 :]):
        target[...] = source[...]


def per_device(tokens, out_grad, expert_ids, gate_probs, w_gate, w_up, w_down):
    E = lax.axis_size("expert")
    T = lax.axis_size("tensor")
    A, B = grid_of(E)
    C, S = CORES, PIECES
    group, feats = tokens.shape
    width = feats * T
    hidden = w_gate.shape[2]
    rows = E * group
    lanes = -(-E // LANES) * LANES
    bf, f32 = jnp.bfloat16, jnp.float32
    pair = (2 * group, feats // (PATHS * PIECES))
    tile = (group, lanes)
    na, nb, nt = A - 1, B - 1, T - 1
    gather = S * 2 * (na + nb + nt + 1) + S * (nb + nt) + na + nb + 1
    scatter = S * 2 * (T + nb + nt + na) + 1 + nt + nb + na
    count = gather + scatter

    def vm(*shape, dtype=bf):
        return pltpu.VMEM(shape, dtype)

    scratch = [
        vm(width, hidden), vm(width, hidden), vm(hidden, width),
        vm(S, C, T, B, A, *pair), vm(S, C, B, T, A, *pair), vm(C, B, A, *tile, dtype=f32),
        vm(rows, width), vm(rows, width),
        vm(rows, hidden), vm(rows, hidden), vm(rows, hidden),
        vm(rows, hidden, dtype=f32), vm(rows, hidden, dtype=f32), vm(rows, hidden, dtype=f32),
        vm(S, C, T, B, A, *pair), vm(S, C, T, B, A, *pair),
        vm(S, T, B, A, *pair), vm(S, T, B, A, *pair),
        vm(S, T, B, A, *pair), vm(S, B, T, A, *pair),
        vm(S, nt, B, A, *pair), vm(S, nb, T, A, *pair),
        vm(S, B, A, *pair), vm(S, T, A, *pair),
        vm(S, nb, A, *pair), vm(S, nt, A, *pair),
        vm(S, A, *pair), vm(S, A, *pair),
        vm(S, na, *pair), vm(S, na, *pair),
        vm(C, B, A, *tile, dtype=f32), vm(B, A, *tile, dtype=f32),
        vm(T, B, A, *tile, dtype=f32), vm(B, A, *tile, dtype=f32),
        vm(nb, A, *tile, dtype=f32), vm(A, *tile, dtype=f32),
        vm(na, *tile, dtype=f32),
        pltpu.SemaphoreType.DMA((3,)),
        pltpu.SemaphoreType.DMA((count,)),
        pltpu.SemaphoreType.DMA((count,)),
    ]
    inside = pl.BlockSpec(memory_space=pltpu.VMEM)
    outside = pl.BlockSpec(memory_space=pl.ANY)
    shapes = (
        jax.ShapeDtypeStruct((group, feats), bf),
        jax.ShapeDtypeStruct((group, feats), bf),
        jax.ShapeDtypeStruct(expert_ids.shape, f32),
    )
    results = pl.pallas_call(
        functools.partial(kernel, A, B, T, count),
        out_shape=shapes,
        in_specs=[inside] * 4 + [outside] * 3,
        out_specs=(inside, inside, inside),
        scratch_shapes=scratch,
        compiler_params=pltpu.CompilerParams(
            collective_id=0, has_side_effects=True, vmem_limit_bytes=60 * 1024 * 1024
        ),
        cost_estimate=pl.CostEstimate(
            flops=12 * rows * width * hidden,
            bytes_accessed=6 * width * hidden,
            transcendentals=rows * hidden,
        ),
    )(tokens, out_grad, expert_ids, gate_probs, w_gate, w_up, w_down)
    return pl.pallas_call(
        settle, out_shape=shapes, in_specs=[inside] * 3, out_specs=(inside, inside, inside)
    )(*results)


def solution(mesh):
    placed = (
        P("expert", "tensor"),
        P("expert", "tensor"),
        P("expert", None),
        P("expert", None),
        P("expert", None, "tensor"),
        P("expert", None, "tensor"),
        P("expert", "tensor", None),
    )
    return jax.shard_map(
        per_device,
        mesh=mesh,
        in_specs=placed,
        out_specs=(P("expert", "tensor"), P("expert", "tensor"), P("expert", None)),
        check_vma=False,
    )
```

time: 46.5 us -> 42.3 us (0.910)
  local copies, waits for them, and re-layouts: 3.92 us -> 0 us
    unnamed x3 -> x0, local copies, waits for them, and re-layouts: 3.92 us -> none
    pallas_call x1 -> x2, Pallas kernels: 41.5 us -> 41.4 us  [the longest x1 40 us: per_device(): pl.pallas_call(functools.partial(kernel, A, B, T, count), out_shape=shape...]
where the time goes in v2:
time: 42.3 us; the launch traced here: 42 us
  Pallas kernels  41.4 us (98%)
  between operations  0.64 us (2%)
    pallas_call x1, Pallas kernels, per_device(): pl.pallas_call(functools.partial(kernel, A, B, T, count), out_shape=shape...  40 us
    pallas_call x1, Pallas kernels, per_device(): pl.pallas_call(settle, out_shape=shapes, in_specs=[inside] * 3, out_specs...  1.35 us

profile of v2, /device:TPU:0, one launch (start us, length us, event | category | flops | bytes accessed | tf_op | source)
XLA Modules:
  0.0 42.0 jit_solution(9353433136224650286)
XLA Ops:
  0.6 40.0 %shard_map.94 = (bf16[8,1024]{1,0:T(8,128)(2,1)}, bf16[8,1024]{1,0:T(8,128)(2,1)}, f32[8,8]{1,0:T(8,128)}) custom-call(bf16[8,1024]{1,0:T(8,128)(2,1)} %tok_ref.1, bf16[8,1024]{1,0:T(8,128)(2,1)} %grad_ref.1, s32[8,8]{1,0:T(8,128)} %ids_ref.1, f32[8,8]{1,0:T(8,128)} %prob_ref.1, bf16[1,2048,768]{2,1,0:T(8,128)(2,1)} %wg_hbm.1, bf16[1,2048,768]{2,1,0:T(8,128)(2,1)} %wu_hbm.1, ...), custom_call_target="tpu_custom_call" | custom-call | flops 2415919104 | bytes 9437184 | tf_op jit(solution)/shard_map/pallas_call | solution.py:441
  40.6 1.4 %shard_map.95 = (bf16[8,1024]{1,0:T(8,128)(2,1)}, bf16[8,1024]{1,0:T(8,128)(2,1)}, f32[8,8]{1,0:T(8,128)}) custom-call(bf16[8,1024]{1,0:T(8,128)(2,1)} %get-tuple-element.6.refs_0_, bf16[8,1024]{1,0:T(8,128)(2,1)} %get-tuple-element.7.refs_1_, f32[8,8]{1,0:T(8,128)} %get-tuple-element.8.refs_2_), custom_call_target="tpu_custom_call" | custom-call | tf_op jit(solution)/shard_map/pallas_call | solution.py:456

commit v3 on v2

--- a/solution.py
+++ b/solution.py
@@ -154,7 +154,7 @@
             here = pl.ds(slot * piece, width * piece)
             there = pl.ds(start, width * piece)
             x, o = xs[at, here], og[at, here]
-            terms = dot_nn(x, wg[there, :]), dot_nn(x, wu[there, :]), dot_nt(o, wd[:, there])
+            terms = dot_nn(x, wg[there, :]), dot_nn(x, wu[there, :]), dot_nt(wd[:, there], o)
             if gate is None:
                 gate, up, back = terms
             else:
@@ -199,7 +199,7 @@
     runs = plan([(0, s, 0, 1) for s in pieces])
 
     def begin(at):
-        sum_gate[at, :], sum_up[at, :], sum_back[at, :] = products(at, runs)
+        sum_gate[at, :], sum_up[at, :], sum_back[:, at] = products(at, runs)
 
     by_rows(begin)
     for s in pieces:
@@ -217,7 +217,7 @@
         gate, up, back = products(at, more)
         gate = gate + sum_gate[at, :]
         up = up + sum_up[at, :]
-        back = back + sum_back[at, :]
+        back = (back + sum_back[:, at]).T
         weights = pg.reshape(rows, lanes)[at, :]
         mine = lax.broadcasted_iota(jnp.int32, (step, lanes), 1) == me
         weight = jnp.sum(jnp.where(mine, weights, 0.0), axis=1, keepdims=True)
@@ -244,7 +244,7 @@
         for i in range(cuts):
             at = pl.ds(i * size, size)
             out = dot_nn(hid[at, :], wd[:, cols])
-            back = dot_nt(gga[at, :], wg[cols, :]) + dot_nt(gup[at, :], wu[cols, :])
+            back = (dot_nt(wg[cols, :], gga[at, :]) + dot_nt(wu[cols, :], gup[at, :])).T
             shape = (CORES // cuts, B, A, group, piece)
             block = jnp.concatenate([out.reshape(shape), back.reshape(shape)], axis=3)
             block = block.astype(jnp.bfloat16)
@@ -414,7 +414,7 @@
         vm(S, C, T, B, A, *pair), vm(S, C, B, T, A, *pair), vm(C, B, A, *tile, dtype=f32),
         vm(rows, width), vm(rows, width),
         vm(rows, hidden), vm(rows, hidden), vm(rows, hidden),
-        vm(rows, hidden, dtype=f32), vm(rows, hidden, dtype=f32), vm(rows, hidden, dtype=f32),
+        vm(rows, hidden, dtype=f32), vm(rows, hidden, dtype=f32), vm(hidden, rows, dtype=f32),
         vm(S, C, T, B, A, *pair), vm(S, C, T, B, A, *pair),
         vm(S, T, B, A, *pair), vm(S, T, B, A, *pair),
         vm(S, T, B, A, *pair), vm(S, B, T, A, *pair),

time: 42.3 us -> 43.1 us (1.019)
  Pallas kernels: 41.4 us -> 42.1 us
    pallas_call x1, Pallas kernels: 40 us -> 40.7 us  [per_device(): pl.pallas_call(functools.partial(kernel, A, B, T, count), out_shape=shape...]
where the time goes in v3:
time: 43.1 us; the launch traced here: 42.7 us
  Pallas kernels  42.1 us (98%)
  between operations  0.64 us (1%)
    pallas_call x1, Pallas kernels, per_device(): pl.pallas_call(functools.partial(kernel, A, B, T, count), out_shape=shape...  40.7 us
    pallas_call x1, Pallas kernels, per_device(): pl.pallas_call(settle, out_shape=shapes, in_specs=[inside] * 3, out_specs...  1.35 us

profile of v3, /device:TPU:0, one launch (start us, length us, event | category | flops | bytes accessed | tf_op | source)
XLA Modules:
  0.0 42.7 jit_solution(9501352237970067195)
XLA Ops:
  0.6 40.7 %shard_map.94 = (bf16[8,1024]{1,0:T(8,128)(2,1)}, bf16[8,1024]{1,0:T(8,128)(2,1)}, f32[8,8]{1,0:T(8,128)}) custom-call(bf16[8,1024]{1,0:T(8,128)(2,1)} %tok_ref.1, bf16[8,1024]{1,0:T(8,128)(2,1)} %grad_ref.1, s32[8,8]{1,0:T(8,128)} %ids_ref.1, f32[8,8]{1,0:T(8,128)} %prob_ref.1, bf16[1,2048,768]{2,1,0:T(8,128)(2,1)} %wg_hbm.1, bf16[1,2048,768]{2,1,0:T(8,128)(2,1)} %wu_hbm.1, ...), custom_call_target="tpu_custom_call" | custom-call | flops 2415919104 | bytes 9437184 | tf_op jit(solution)/shard_map/pallas_call | solution.py:441
  41.4 1.4 %shard_map.95 = (bf16[8,1024]{1,0:T(8,128)(2,1)}, bf16[8,1024]{1,0:T(8,128)(2,1)}, f32[8,8]{1,0:T(8,128)}) custom-call(bf16[8,1024]{1,0:T(8,128)(2,1)} %get-tuple-element.6.refs_0_, bf16[8,1024]{1,0:T(8,128)(2,1)} %get-tuple-element.7.refs_1_, f32[8,8]{1,0:T(8,128)} %get-tuple-element.8.refs_2_), custom_call_target="tpu_custom_call" | custom-call | tf_op jit(solution)/shard_map/pallas_call | solution.py:456

commit v4 on v2

--- a/solution.py
+++ b/solution.py
@@ -37,9 +37,9 @@
     tok_ref, grad_ref, ids_ref, prob_ref, wg_hbm, wu_hbm, wd_hbm,
     mixed_ref, tgrad_ref, pgrad_ref,
     wg, wu, wd, g0, g1, pg, xs, og, hid, gga, gup, sum_gate, sum_up, sum_back,
-    r0, r1, rc0, rc1, s0, s1, rx0, ry1, u0, u1, ry0, rx1, v0, v1, rz0, rz1,
+    rr, rc, s0, s1, rx0, ry1, u0, u1, ry0, rx1, v0, v1, rz0, rz1,
     qr, qc, qx, qt, qy, qv, qz,
-    wsem, ssem, rsem,
+    wsem, ssem, rsem, csend, crecv,
 ):
     me = lax.axis_index("expert")
     t = lax.axis_index("tensor")
@@ -95,13 +95,19 @@
 
     started = []
 
+    def view(part):
+        return part[0].at[part[1]]
+
     def send(src, dst, peer):
         i = len(started)
-        copy = pltpu.make_async_remote_copy(
-            src_ref=src, dst_ref=dst, send_sem=ssem.at[i], recv_sem=rsem.at[i],
-            device_id=peer, device_id_type=MESH,
-        )
-        copy.start()
+
+        def copy():
+            return pltpu.make_async_remote_copy(
+                src_ref=view(src), dst_ref=view(dst), send_sem=ssem.at[i], recv_sem=rsem.at[i],
+                device_id=peer, device_id_type=MESH,
+            )
+
+        copy().start()
         started.append(copy)
         return copy
 
@@ -110,30 +116,30 @@
 
     def arrive(copies):
         for copy in copies:
-            copy.wait_recv()
+            copy().wait_recv()
 
     a0, a1, b0, b1, c0, c1 = ([None] * PIECES for _ in range(6))
     for s in pieces:
-        a0[s] = same(g0.at[s, c, t, b, a], to_a)
-        a1[s] = same(g1.at[s, c, b, t, a], to_a)
-    ap = same(pg.at[c, b, a], to_a)
+        a0[s] = same((g0, (s, c, t, b, a,)), to_a)
+        a1[s] = same((g1, (s, c, b, t, a,)), to_a)
+    ap = same((pg, (c, b, a,)), to_a)
     for s in pieces:
         arrive(a0[s])
-        b0[s] = same(g0.at[s, c, t, b], to_b)
+        b0[s] = same((g0, (s, c, t, b,)), to_b)
         arrive(a1[s])
-        b1[s] = same(g1.at[s, c, b, t], to_t)
+        b1[s] = same((g1, (s, c, b, t,)), to_t)
     arrive(ap)
-    bp = same(pg.at[c, b], to_b)
+    bp = same((pg, (c, b,)), to_b)
     own, rest0, rest1 = [], [], []
     for s in pieces:
         arrive(b0[s])
-        c0[s] = same(g0.at[s, c, t], to_t)
-        own += same(g0.at[s, c, t], [to_c])
+        c0[s] = same((g0, (s, c, t,)), to_t)
+        own += same((g0, (s, c, t,)), [to_c])
         arrive(b1[s])
-        c1[s] = same(g1.at[s, c, b], to_b)
-        rest1.append(same(g1.at[s, c, b], [to_c]))
+        c1[s] = same((g1, (s, c, b,)), to_b)
+        rest1.append(same((g1, (s, c, b,)), [to_c]))
     arrive(bp)
-    dp = same(pg.at[c], [to_c])
+    dp = same((pg, (c,)), [to_c])
 
     part = B * A * group
     step = min(rows, 256)
@@ -147,14 +153,21 @@
             xs[at] = block[:, :, :group].reshape(part, piece).astype(jnp.bfloat16)
             og[at] = block[:, :, group:].reshape(part, piece).astype(jnp.bfloat16)
 
-    def products(at, runs):
+    wide_tile = 256 if hid.shape[1] % 256 == 0 else 128
+    tiles = hid.shape[1] // wide_tile
+
+    def tile_at(n):
+        return pl.ds(pl.multiple_of(n * wide_tile, wide_tile), wide_tile)
+
+    def products(at, runs, cols):
         gate = up = back = None
-        for slot, h, s, r, width in runs:
-            start = pl.multiple_of(turn(t, r, T) * feats + column(h, s), piece)
+        for slot, start, width in runs:
             here = pl.ds(slot * piece, width * piece)
             there = pl.ds(start, width * piece)
             x, o = xs[at, here], og[at, here]
-            terms = dot_nn(x, wg[there, :]), dot_nn(x, wu[there, :]), dot_nt(o, wd[:, there])
+            terms = (
+                dot_nn(x, wg[there, cols]), dot_nn(x, wu[there, cols]), dot_nt(o, wd[cols, there])
+            )
             if gate is None:
                 gate, up, back = terms
             else:
@@ -178,19 +191,20 @@
         for h, s, r, width in runs:
             for i in range(width):
                 assemble(slots + i, h + i, s, r)
-            out.append((slots, h, s, r, width))
+            start = pl.multiple_of(turn(t, r, T) * feats + column(h, s), piece)
+            out.append((slots, start, width))
             slots += width
         return out
 
     def forward0(s):
         for r in range(1, T):
-            c0[s][r - 1].wait_recv()
-            rest0.append(same(g0.at[s, c, turn(t, T - r, T)], [to_c]))
+            c0[s][r - 1]().wait_recv()
+            rest0.append(same((g0, (s, c, turn(t, T - r, T),)), [to_c]))
 
     def forward1(s):
         for r in range(1, B):
-            c1[s][r - 1].wait_recv()
-            rest1.append(same(g1.at[s, c, turn(b, B - r, B)], [to_c]))
+            c1[s][r - 1]().wait_recv()
+            rest1.append(same((g1, (s, c, turn(b, B - r, B),)), [to_c]))
 
     forward0(0)
     for load in loads:
@@ -199,7 +213,10 @@
     runs = plan([(0, s, 0, 1) for s in pieces])
 
     def begin(at):
-        sum_gate[at, :], sum_up[at, :], sum_back[at, :] = products(at, runs)
+        @pl.loop(0, tiles)
+        def _(n):
+            cols = tile_at(n)
+            sum_gate[at, cols], sum_up[at, cols], sum_back[at, cols] = products(at, runs, cols)
 
     by_rows(begin)
     for s in pieces:
@@ -214,32 +231,56 @@
     )
 
     def finish(at):
-        gate, up, back = products(at, more)
-        gate = gate + sum_gate[at, :]
-        up = up + sum_up[at, :]
-        back = back + sum_back[at, :]
         weights = pg.reshape(rows, lanes)[at, :]
         mine = lax.broadcasted_iota(jnp.int32, (step, lanes), 1) == me
         weight = jnp.sum(jnp.where(mine, weights, 0.0), axis=1, keepdims=True)
-        sig = jax.nn.sigmoid(gate)
-        silu = gate * sig
-        hidden = silu * up
-        inner = jnp.sum(hidden * back, axis=1, keepdims=True)
-        back = back * weight
-        hid[at, :] = (hidden * weight).astype(jnp.bfloat16)
-        gga[at, :] = (back * up * sig * (1.0 + gate * (1.0 - sig))).astype(jnp.bfloat16)
-        gup[at, :] = (back * silu).astype(jnp.bfloat16)
+
+        def tile(n, inner):
+            cols = tile_at(n)
+            gate, up, back = products(at, more, cols)
+            gate = gate + sum_gate[at, cols]
+            up = up + sum_up[at, cols]
+            back = back + sum_back[at, cols]
+            sig = jax.nn.sigmoid(gate)
+            silu = gate * sig
+            hidden = silu * up
+            inner = inner + jnp.sum(hidden * back, axis=1, keepdims=True)
+            back = back * weight
+            hid[at, cols] = (hidden * weight).astype(jnp.bfloat16)
+            gga[at, cols] = (back * up * sig * (1.0 + gate * (1.0 - sig))).astype(jnp.bfloat16)
+            gup[at, cols] = (back * silu).astype(jnp.bfloat16)
+            return inner
+
+        inner = lax.fori_loop(0, tiles, tile, jnp.zeros((step, 1), jnp.float32))
         qr.reshape(rows, lanes)[at, :] = jnp.where(mine, inner, 0.0)
 
     by_rows(finish)
-    ec = send(qr.at[1 - c], qc, to_c)
+    ec = send((qr, (1 - c,)), (qc, ()), to_c)
 
     cuts = CORES if rows > 256 else 1
 
-    def second(h, s, r):
-        tt = turn(t, r, T)
-        ref, landing = ((r0, rc0), (r1, rc1))[h]
-        cols = pl.ds(pl.multiple_of(tt * feats + column(h, s), piece), piece)
+    blocks = PATHS * T * PIECES
+    tts = [turn(t, r, T) for r in range(T)]
+    bbs = [turn(b, r, B) for r in range(B)]
+    aas = [turn(a, r, A) for r in range(A)]
+
+    def to_core(h, s, tt, q):
+        return pltpu.make_async_remote_copy(
+            src_ref=rr.at[h, s, 1 - c, tt], dst_ref=rc.at[h, s, tt],
+            send_sem=csend.at[q], recv_sem=crecv.at[q],
+            device_id=to_c, device_id_type=MESH,
+        )
+
+    def order(h, s, r):
+        return (s * T + (r + T - 1) % T) * PATHS + h
+
+    def second(q):
+        h = lax.rem(q, PATHS)
+        turns = lax.div(q, PATHS)
+        s = lax.div(turns, T)
+        tt = lax.rem(t + 1 + lax.rem(turns, T), T)
+        start = tt * feats + (s * PATHS + h) * piece
+        cols = pl.ds(pl.multiple_of(start, piece), piece)
         size = rows // cuts
         for i in range(cuts):
             at = pl.ds(i * size, size)
@@ -249,8 +290,11 @@
             block = jnp.concatenate([out.reshape(shape), back.reshape(shape)], axis=3)
             block = block.astype(jnp.bfloat16)
             for j in range(CORES // cuts):
-                ref[s, i + j, tt] = block[j]
-        return send(ref.at[s, 1 - c, tt], landing.at[s, tt], to_c)
+                rr[h, s, i + j, tt] = block[j]
+        to_core(h, s, tt, q).start()
+
+    def core_came(h, s, r):
+        to_core(h, s, tts[r], order(h, s, r)).wait_recv()
 
     def wide(value):
         return value.astype(jnp.float32)
@@ -264,97 +308,98 @@
             value = value + wide(ref[i])
         return value
 
-    far = list(range(1, T))
-    e0 = [[None] * T for _ in pieces]
-    e1 = [[None] * T for _ in pieces]
     f0, f1, h0, h1, k0, k1 = ([None] * PIECES for _ in range(6))
+    late = {}
 
     def away0(s):
         f0[s] = []
-        for r in far:
-            e0[s][r].wait_recv()
-            tt = turn(t, r, T)
-            s0[s, tt] = narrow(wide(r0[s, c, tt]) + wide(rc0[s, tt]))
-            f0[s].append(send(s0.at[s, tt], rx0.at[s, r - 1], to_t[r - 1]))
+        for r in range(1, T):
+            core_came(0, s, r)
+            tt = tts[r]
+            s0[s, tt] = narrow(wide(rr[0, s, c, tt]) + wide(rc[0, s, tt]))
+            f0[s].append(send((s0, (s, tt,)), (rx0, (s, r - 1,)), to_t[r - 1]))
 
     def home0(s):
-        e0[s][0].wait_recv()
-        s0[s, t] = narrow(wide(r0[s, c, t]) + wide(rc0[s, t]))
+        core_came(0, s, 0)
+        s0[s, t] = narrow(wide(rr[0, s, c, t]) + wide(rc[0, s, t]))
 
     def away1(s):
-        arrive(e1[s])
+        for r in range(T):
+            core_came(1, s, r)
         f1[s] = []
         for r in list(range(1, B)) + [0]:
-            bb = turn(b, r, B)
-            s1[s, bb] = narrow(wide(r1[s, c, :, bb]) + wide(rc1[s, :, bb]))
+            bb = bbs[r]
+            s1[s, bb] = narrow(wide(rr[1, s, c, :, bb]) + wide(rc[1, s, :, bb]))
             if r:
-                f1[s].append(send(s1.at[s, bb], ry1.at[s, r - 1], to_b[r - 1]))
+                f1[s].append(send((s1, (s, bb,)), (ry1, (s, r - 1,)), to_b[r - 1]))
 
     def across0(s):
         arrive(f0[s])
         u0[s] = narrow(total(s0[s, t], rx0.at[s]))
-        h0[s] = [
-            send(u0.at[s, turn(b, r, B)], ry0.at[s, r - 1], to_b[r - 1]) for r in range(1, B)
-        ]
+        h0[s] = [send((u0, (s, bbs[r],)), (ry0, (s, r - 1,)), to_b[r - 1]) for r in range(1, B)]
 
     def across1(s):
         arrive(f1[s])
         u1[s] = narrow(total(s1[s, b], ry1.at[s]))
-        h1[s] = [
-            send(u1.at[s, turn(t, r, T)], rx1.at[s, r - 1], to_t[r - 1]) for r in range(1, T)
-        ]
+        h1[s] = [send((u1, (s, tts[r],)), (rx1, (s, r - 1,)), to_t[r - 1]) for r in range(1, T)]
 
     def along0(s):
         arrive(h0[s])
         v0[s] = narrow(total(u0[s, b], ry0.at[s]))
-        k0[s] = [
-            send(v0.at[s, turn(a, r, A)], rz0.at[s, r - 1], to_a[r - 1]) for r in range(1, A)
-        ]
+        k0[s] = [send((v0, (s, aas[r],)), (rz0, (s, r - 1,)), to_a[r - 1]) for r in range(1, A)]
 
     def along1(s):
         arrive(h1[s])
         v1[s] = narrow(total(u1[s, t], rx1.at[s]))
-        k1[s] = [
-            send(v1.at[s, turn(a, r, A)], rz1.at[s, r - 1], to_a[r - 1]) for r in range(1, A)
-        ]
-
-    for s in pieces:
-        for r in far:
-            e0[s][r] = second(0, s, r)
-        if s:
-            home0(s - 1)
-        for r in far:
-            e1[s][r] = second(1, s, r)
-        away0(s)
-        if s:
-            across0(s - 1)
-        else:
-            ec.wait_recv()
-            qx[t] = qr[c] + qc[...]
-            fq = same(qx.at[t], to_t)
-        e1[s][0] = second(1, s, 0)
-        e0[s][0] = second(0, s, 0)
-        away1(s)
+        k1[s] = [send((v1, (s, aas[r],)), (rz1, (s, r - 1,)), to_a[r - 1]) for r in range(1, A)]
+
+    def inner0():
+        ec().wait_recv()
+        qx[t] = qr[c] + qc[...]
+        late["t"] = same((qx, (t,)), to_t)
+
+    def inner1():
+        arrive(late["t"])
+        value = qx[0]
+        for i in range(1, T):
+            value = value + qx[i]
+        qt[...] = value
+        late["b"] = [send((qt, (bbs[r],)), (qy, (r - 1,)), to_b[r - 1]) for r in range(1, B)]
+
+    def inner2():
+        arrive(late["b"])
+        qv[...] = total(qt[b], qy)
+        late["a"] = [send((qv, (aas[r],)), (qz, (r - 1,)), to_a[r - 1]) for r in range(1, A)]
+
+    each = PATHS * T
+    tasks = [(1, 0, inner0, ()), (each, 0, inner1, ()), (each + 2, 0, inner2, ())]
+    for s in range(PIECES):
+        base = s * each
+        tasks.append((base + each - 2, 1, away0, (s,)))
+        tasks.append((base + each, 2, away1, (s,)))
+        tasks.append((base + each, 3, home0, (s,)))
+        tasks.append((base + each + 1, 4, across0, (s,)))
+        tasks.append((base + each + 2, 5, across1, (s,)))
+        tasks.append((base + each + 3, 6, along0, (s,)))
+        tasks.append((base + each + 4, 7, along1, (s,)))
+    tasks.sort(key=lambda task: task[:2])
+
+    @pl.loop(0, blocks)
+    def _(q):
+        second(q)
+        for k in range(blocks):
+            now = [task for task in tasks if task[0] == k]
+            if now:
+
+                @pl.when(q == k)
+                def _():
+                    for task in now:
+                        task[2](*task[3])
+
+    for task in tasks:
+        if task[0] >= blocks:
+            task[2](*task[3])
     last = PIECES - 1
-    for s in range(last):
-        across1(s)
-    home0(last)
-    arrive(fq)
-    value = qx[0]
-    for i in range(1, T):
-        value = value + qx[i]
-    qt[...] = value
-    hq = [send(qt.at[turn(b, r, B)], qy.at[r - 1], to_b[r - 1]) for r in range(1, B)]
-    for s in range(last):
-        along0(s)
-    across0(last)
-    arrive(hq)
-    qv[...] = total(qt[b], qy)
-    kq = [send(qv.at[turn(a, r, A)], qz.at[r - 1], to_a[r - 1]) for r in range(1, A)]
-    for s in range(last):
-        along1(s)
-    across1(last)
-    along0(last)
 
     def deliver(h, s, mine, ref, copies):
         arrive(copies)
@@ -365,7 +410,7 @@
 
     for s in range(last):
         deliver(0, s, v0[s, a], rz0.at[s], k0[s])
-    arrive(kq)
+    arrive(late["a"])
     inner = total(qv[a], qz)
     place = lax.broadcasted_iota(jnp.int32, ids.shape, 1)
     result = jnp.zeros(ids.shape, jnp.float32)
@@ -373,14 +418,17 @@
         one = jnp.sum(jnp.where(lane == ids[:, k : k + 1], inner, 0.0), axis=1, keepdims=True)
         result = jnp.where(place == k, one, result)
     pgrad_ref[...] = result
-    along1(last)
     for s in range(last):
         deliver(1, s, v1[s, a], rz1.at[s], k1[s])
     deliver(0, last, v0[last, a], rz0.at[last], k0[last])
     deliver(1, last, v1[last, a], rz1.at[last], k1[last])
     assert len(started) == count
     for copy in started:
-        copy.wait_send()
+        copy().wait_send()
+    for s in pieces:
+        for h in range(PATHS):
+            for r in range(T):
+                to_core(h, s, tts[r], order(h, s, r)).wait_send()
 
 
 def settle(*refs):
@@ -403,7 +451,7 @@
     tile = (group, lanes)
     na, nb, nt = A - 1, B - 1, T - 1
     gather = S * 2 * (na + nb + nt + 1) + S * (nb + nt) + na + nb + 1
-    scatter = S * 2 * (T + nb + nt + na) + 1 + nt + nb + na
+    scatter = S * 2 * (nb + nt + na) + 1 + nt + nb + na
     count = gather + scatter
 
     def vm(*shape, dtype=bf):
@@ -415,8 +463,7 @@
         vm(rows, width), vm(rows, width),
         vm(rows, hidden), vm(rows, hidden), vm(rows, hidden),
         vm(rows, hidden, dtype=f32), vm(rows, hidden, dtype=f32), vm(rows, hidden, dtype=f32),
-        vm(S, C, T, B, A, *pair), vm(S, C, T, B, A, *pair),
-        vm(S, T, B, A, *pair), vm(S, T, B, A, *pair),
+        vm(PATHS, S, C, T, B, A, *pair), vm(PATHS, S, T, B, A, *pair),
         vm(S, T, B, A, *pair), vm(S, B, T, A, *pair),
         vm(S, nt, B, A, *pair), vm(S, nb, T, A, *pair),
         vm(S, B, A, *pair), vm(S, T, A, *pair),
@@ -430,6 +477,8 @@
         pltpu.SemaphoreType.DMA((3,)),
         pltpu.SemaphoreType.DMA((count,)),
         pltpu.SemaphoreType.DMA((count,)),
+        pltpu.SemaphoreType.DMA((PATHS * S * T,)),
+        pltpu.SemaphoreType.DMA((PATHS * S * T,)),
     ]
     inside = pl.BlockSpec(memory_space=pltpu.VMEM)
     outside = pl.BlockSpec(memory_space=pl.ANY)

time: 42.3 us -> 44.6 us (1.054)
  Pallas kernels: 41.4 us -> 43.6 us
    pallas_call x1, Pallas kernels: 40 us -> 42.3 us  [per_device(): pl.pallas_call(functools.partial(kernel, A, B, T, count), out_shape=shape...]
where the time goes in v4:
time: 44.6 us; the launch traced here: 44.3 us
  Pallas kernels  43.6 us (98%)
  between operations  0.64 us (1%)
    pallas_call x1, Pallas kernels, per_device(): pl.pallas_call(functools.partial(kernel, A, B, T, count), out_shape=shape...  42.3 us
    pallas_call x1, Pallas kernels, per_device(): pl.pallas_call(settle, out_shape=shapes, in_specs=[inside] * 3, out_specs...  1.35 us

profile of v4, /device:TPU:0, one launch (start us, length us, event | category | flops | bytes accessed | tf_op | source)
XLA Modules:
  0.0 44.3 jit_solution(13728996260551219916)
XLA Ops:
  0.6 42.3 %shard_map.94 = (bf16[8,1024]{1,0:T(8,128)(2,1)}, bf16[8,1024]{1,0:T(8,128)(2,1)}, f32[8,8]{1,0:T(8,128)}) custom-call(bf16[8,1024]{1,0:T(8,128)(2,1)} %tok_ref.1, bf16[8,1024]{1,0:T(8,128)(2,1)} %grad_ref.1, s32[8,8]{1,0:T(8,128)} %ids_ref.1, f32[8,8]{1,0:T(8,128)} %prob_ref.1, bf16[1,2048,768]{2,1,0:T(8,128)(2,1)} %wg_hbm.1, bf16[1,2048,768]{2,1,0:T(8,128)(2,1)} %wu_hbm.1, ...), custom_call_target="tpu_custom_call" | custom-call | flops 2415919104 | bytes 9437184 | tf_op jit(solution)/shard_map/pallas_call | solution.py:490
  42.9 1.4 %shard_map.95 = (bf16[8,1024]{1,0:T(8,128)(2,1)}, bf16[8,1024]{1,0:T(8,128)(2,1)}, f32[8,8]{1,0:T(8,128)}) custom-call(bf16[8,1024]{1,0:T(8,128)(2,1)} %get-tuple-element.6.refs_0_, bf16[8,1024]{1,0:T(8,128)(2,1)} %get-tuple-element.7.refs_1_, f32[8,8]{1,0:T(8,128)} %get-tuple-element.8.refs_2_), custom_call_target="tpu_custom_call" | custom-call | tf_op jit(solution)/shard_map/pallas_call | solution.py:505

commit v5 on v2

--- a/solution.py
+++ b/solution.py
@@ -10,7 +10,7 @@
 CORES = 2
 LANES = 128
 PATHS = 2
-PIECES = 2
+PIECES = 1
 MESH = pl.DeviceIdType.MESH
 
 

time: 42.3 us -> 43.3 us (1.024)
  Pallas kernels: 41.4 us -> 42.3 us
    pallas_call x1, Pallas kernels: 40 us -> 40.9 us  [per_device(): pl.pallas_call(functools.partial(kernel, A, B, T, count), out_shape=shape...]
where the time goes in v5:
time: 43.3 us; the launch traced here: 42.9 us
  Pallas kernels  42.3 us (98%)
  between operations  0.64 us (1%)
    pallas_call x1, Pallas kernels, per_device(): pl.pallas_call(functools.partial(kernel, A, B, T, count), out_shape=shape...  40.9 us
    pallas_call x1, Pallas kernels, per_device(): pl.pallas_call(settle, out_shape=shapes, in_specs=[inside] * 3, out_specs...  1.35 us

profile of v5, /device:TPU:0, one launch (start us, length us, event | category | flops | bytes accessed | tf_op | source)
XLA Modules:
  0.0 42.9 jit_solution(15882198333717245786)
XLA Ops:
  0.6 40.9 %shard_map.94 = (bf16[8,1024]{1,0:T(8,128)(2,1)}, bf16[8,1024]{1,0:T(8,128)(2,1)}, f32[8,8]{1,0:T(8,128)}) custom-call(bf16[8,1024]{1,0:T(8,128)(2,1)} %tok_ref.1, bf16[8,1024]{1,0:T(8,128)(2,1)} %grad_ref.1, s32[8,8]{1,0:T(8,128)} %ids_ref.1, f32[8,8]{1,0:T(8,128)} %prob_ref.1, bf16[1,2048,768]{2,1,0:T(8,128)(2,1)} %wg_hbm.1, bf16[1,2048,768]{2,1,0:T(8,128)(2,1)} %wu_hbm.1, ...), custom_call_target="tpu_custom_call" | custom-call | flops 2415919104 | bytes 9437184 | tf_op jit(solution)/shard_map/pallas_call | solution.py:441
  41.6 1.4 %shard_map.95 = (bf16[8,1024]{1,0:T(8,128)(2,1)}, bf16[8,1024]{1,0:T(8,128)(2,1)}, f32[8,8]{1,0:T(8,128)}) custom-call(bf16[8,1024]{1,0:T(8,128)(2,1)} %get-tuple-element.6.refs_0_, bf16[8,1024]{1,0:T(8,128)(2,1)} %get-tuple-element.7.refs_1_, f32[8,8]{1,0:T(8,128)} %get-tuple-element.8.refs_2_), custom_call_target="tpu_custom_call" | custom-call | tf_op jit(solution)/shard_map/pallas_call | solution.py:456

commit v6 on v1

v6 whole, which is shorter than its diff:
```python
import functools

import jax
import jax.numpy as jnp
from jax import lax
from jax.experimental import pallas as pl
from jax.experimental.pallas import tpu as pltpu
from jax.sharding import PartitionSpec as P

CORES = 2
LANES = 128
PIECES = 2
MESH = pl.DeviceIdType.MESH


def grid_of(expert_count):
    chips = expert_count // CORES
    fast = 1
    while (fast * 2) * (fast * 2) <= chips:
        fast *= 2
    return chips // fast, fast


def dot_nn(left, right):
    return jnp.dot(left, right, preferred_element_type=jnp.float32)


def dot_nt(left, right):
    return lax.dot_general(
        left, right, (((1,), (1,)), ((), ())), preferred_element_type=jnp.float32
    )


def kernel(
    A, B, T, count,
    tok_ref, grad_ref, ids_ref, prob_ref, wg_hbm, wu_hbm, wd_hbm,
    mixed_ref, tgrad_ref, pgrad_ref,
    wg, wu, wd, g, pg, xs, og, hid, gga, gup, sum_gate, sum_up, sum_back,
    parts, landed, sums, rq, v, rz, qr, qc, qx, qv, qz,
    wsem, ssem, rsem,
):
    me = lax.axis_index("expert")
    t = lax.axis_index("tensor")
    c = lax.rem(me, CORES)
    b = lax.rem(lax.div(me, CORES), B)
    a = lax.div(me, CORES * B)
    group, feats = tok_ref.shape
    piece = feats // PIECES
    lanes = pg.shape[-1]
    rows = xs.shape[0]
    pieces = range(PIECES)

    def spot(aa, bb, cc, tt):
        return ((aa * B + bb) * CORES + cc, tt)

    def turn(value, r, size):
        return lax.rem(value + r, size)

    q = t * B + b
    offsets = [(i, j) for i in range(T) for j in range(B) if i or j]
    to_a = [spot(turn(a, r, A), b, c, t) for r in range(1, A)]
    to_b = [spot(a, turn(b, r, B), c, t) for r in range(1, B)]
    to_q = [spot(a, turn(b, j, B), c, turn(t, i, T)) for i, j in offsets]
    to_c = spot(a, b, 1 - c, t)

    loads = [
        pltpu.make_async_copy(src.at[0], dst, wsem.at[i])
        for i, (src, dst) in enumerate(((wg_hbm, wg), (wu_hbm, wu), (wd_hbm, wd)))
    ]

    barrier = pltpu.get_barrier_semaphore()
    peers = to_a + to_q + [to_c]
    for peer in peers:
        pl.semaphore_signal(barrier, inc=1, device_id=peer, device_id_type=MESH)
    for load in loads:
        load.start()

    ids = ids_ref[...]
    probs = prob_ref[...]
    lane = lax.broadcasted_iota(jnp.int32, (group, lanes), 1)
    routed = jnp.zeros((group, lanes), jnp.float32)
    for k in range(ids.shape[1]):
        routed = routed + jnp.where(lane == ids[:, k : k + 1], probs[:, k : k + 1], 0.0)
    unit = jnp.concatenate(
        [tok_ref[...].astype(jnp.float32), grad_ref[...].astype(jnp.float32)], axis=0
    ).astype(jnp.bfloat16)
    for s in pieces:
        g[s, c, q, a] = unit[:, s * piece : (s + 1) * piece]
    pg[c, b, a] = routed
    pl.semaphore_wait(barrier, len(peers))

    started = []

    def send(src, dst, peer):
        i = len(started)
        copy = pltpu.make_async_remote_copy(
            src_ref=src, dst_ref=dst, send_sem=ssem.at[i], recv_sem=rsem.at[i],
            device_id=peer, device_id_type=MESH,
        )
        copy.start()
        started.append(copy)
        return copy

    def same(ref, peers):
        return [send(ref, ref, peer) for peer in peers]

    def arrive(copies):
        for copy in copies:
            copy.wait_recv()

    along = [same(g.at[s, c, q, a], to_a) for s in pieces]
    ap = same(pg.at[c, b, a], to_a)
    across = []
    for s in pieces:
        arrive(along[s])
        across.append(same(g.at[s, c, q], to_q))
    arrive(ap)
    bp = same(pg.at[c, b], to_b)

    part = B * A * group
    step = min(rows, 256)

    def assemble(s):
        for cc in range(CORES):
            for tt in range(T):
                block = g[s, cc, tt * B : (tt + 1) * B].astype(jnp.float32)
                at = (pl.ds(cc * part, part), pl.ds((s * T + tt) * piece, piece))
                xs[at] = block[:, :, :group].reshape(part, piece).astype(jnp.bfloat16)
                og[at] = block[:, :, group:].reshape(part, piece).astype(jnp.bfloat16)

    def products(at, s):
        gate = up = back = None
        for tt in range(T):
            here = pl.ds((s * T + tt) * piece, piece)
            there = pl.ds(tt * feats + s * piece, piece)
            x, o = xs[at, here], og[at, here]
            terms = dot_nn(x, wg[there, :]), dot_nn(x, wu[there, :]), dot_nt(o, wd[:, there])
            if gate is None:
                gate, up, back = terms
            else:
                gate, up, back = gate + terms[0], up + terms[1], back + terms[2]
        return gate, up, back

    def by_rows(body):
        if rows == step:
            body(pl.ds(0, rows))
        else:

            @pl.loop(0, rows // step)
            def _(i):
                body(pl.ds(pl.multiple_of(i * step, step), step))

    def swap(s):
        arrive(across[s])
        return same(g.at[s, c], [to_c])

    came = swap(0)
    arrive(bp)
    dp = same(pg.at[c], [to_c])
    for load in loads:
        load.wait()
    for s in pieces[:-1]:
        arrive(came)
        assemble(s)

        def add(at):
            gate, up, back = products(at, s)
            if s:
                gate = gate + sum_gate[at, :]
                up = up + sum_up[at, :]
                back = back + sum_back[at, :]
            sum_gate[at, :], sum_up[at, :], sum_back[at, :] = gate, up, back

        by_rows(add)
        came = swap(s + 1)
    last = PIECES - 1
    arrive(came)
    arrive(dp)
    assemble(last)

    def finish(at):
        gate, up, back = products(at, last)
        if last:
            gate = gate + sum_gate[at, :]
            up = up + sum_up[at, :]
            back = back + sum_back[at, :]
        weights = pg.reshape(rows, lanes)[at, :]
        mine = lax.broadcasted_iota(jnp.int32, (step, lanes), 1) == me
        weight = jnp.sum(jnp.where(mine, weights, 0.0), axis=1, keepdims=True)
        sig = jax.nn.sigmoid(gate)
        silu = gate * sig
        hidden = silu * up
        inner = jnp.sum(hidden * back, axis=1, keepdims=True)
        back = back * weight
        hid[at, :] = (hidden * weight).astype(jnp.bfloat16)
        gga[at, :] = (back * up * sig * (1.0 + gate * (1.0 - sig))).astype(jnp.bfloat16)
        gup[at, :] = (back * silu).astype(jnp.bfloat16)
        qr.reshape(rows, lanes)[at, :] = jnp.where(mine, inner, 0.0)

    by_rows(finish)
    ec = send(qr.at[1 - c], qc, to_c)

    cuts = CORES if rows > 256 else 1

    def second(s, r):
        tt = turn(t, r, T)
        cols = pl.ds(pl.multiple_of(tt * feats + s * piece, piece), piece)
        size = rows // cuts
        for i in range(cuts):
            at = pl.ds(i * size, size)
            out = dot_nn(hid[at, :], wd[:, cols])
            back = dot_nt(gga[at, :], wg[cols, :]) + dot_nt(gup[at, :], wu[cols, :])
            shape = (CORES // cuts, B, A, group, piece)
            block = jnp.concatenate([out.reshape(shape), back.reshape(shape)], axis=3)
            block = block.astype(jnp.bfloat16)
            for j in range(CORES // cuts):
                parts[s, i + j, tt] = block[j]
        return send(parts.at[s, 1 - c, tt], landed.at[s, tt], to_c)

    def wide(value):
        return value.astype(jnp.float32)

    def narrow(value):
        return value.astype(jnp.bfloat16)

    def total(first_term, ref):
        value = wide(first_term)
        for i in range(ref.shape[0]):
            value = value + wide(ref[i])
        return value

    turns = list(range(1, T)) + [0]
    hops = [[] for _ in pieces]
    ends = [None] * PIECES
    cores = {}

    def hop(s, r):
        cores[s, r].wait_recv()
        tt = turn(t, r, T)
        sums[s, tt] = narrow(wide(parts[s, c, tt]) + wide(landed[s, tt]))
        for i, (rt, rb) in enumerate(offsets):
            if rt == r:
                source = sums.at[s, tt, turn(b, rb, B)]
                hops[s].append(send(source, rq.at[s, i], to_q[i]))

    def home(s):
        arrive(hops[s])
        v[s] = narrow(total(sums[s, t, b], rq.at[s]))
        ends[s] = [
            send(v.at[s, turn(a, r, A)], rz.at[s, r - 1], to_a[r - 1]) for r in range(1, A)
        ]

    before = None
    for s in pieces:
        for r in turns:
            cores[s, r] = second(s, r)
            if before is not None:
                hop(*before)
            else:
                ec.wait_recv()
                qc[...] = qr[c] + qc[...]
                qx[q] = qc[b]
                eq = [
                    send(qc.at[turn(b, j, B)], qx.at[q], peer)
                    for (i, j), peer in zip(offsets, to_q)
                ]
            before = (s, r)
    hop(*before)
    arrive(eq)
    qv[...] = total(qx[0], qx.at[pl.ds(1, T * B - 1)])
    kq = [send(qv.at[turn(a, r, A)], qz.at[r - 1], to_a[r - 1]) for r in range(1, A)]
    for s in pieces:
        home(s)
    for copy in started:
        copy.wait_send()
    arrive(kq)
    inner = total(qv[a], qz)
    place = lax.broadcasted_iota(jnp.int32, ids.shape, 1)
    result = jnp.zeros(ids.shape, jnp.float32)
    for k in range(ids.shape[1]):
        one = jnp.sum(jnp.where(lane == ids[:, k : k + 1], inner, 0.0), axis=1, keepdims=True)
        result = jnp.where(place == k, one, result)
    pgrad_ref[...] = result
    for s in pieces:
        arrive(ends[s])
        value = total(v[s, a], rz.at[s])
        at = pl.ds(s * piece, piece)
        mixed_ref[:, at] = narrow(value[:group])
        tgrad_ref[:, at] = narrow(value[group:])
    assert len(started) == count


def settle(*refs):
    for source, target in zip(refs[: len(refs) // 2], refs[len(refs) // 2 :]):
        target[...] = source[...]


def per_device(tokens, out_grad, expert_ids, gate_probs, w_gate, w_up, w_down):
    E = lax.axis_size("expert")
    T = lax.axis_size("tensor")
    A, B = grid_of(E)
    C, S = CORES, PIECES
    group, feats = tokens.shape
    width = feats * T
    hidden = w_gate.shape[2]
    rows = E * group
    lanes = -(-E // LANES) * LANES
    bf, f32 = jnp.bfloat16, jnp.float32
    pair = (2 * group, feats // PIECES)
    tile = (group, lanes)
    na, nb, nq = A - 1, B - 1, T * B - 1
    gather = S * (na + nq + 1) + na + nb + 1
    scatter = S * (T + nq + na) + 1 + nq + na
    count = gather + scatter

    def vm(*shape, dtype=bf):
        return pltpu.VMEM(shape, dtype)

    scratch = [
        vm(width, hidden), vm(width, hidden), vm(hidden, width),
        vm(S, C, T * B, A, *pair), vm(C, B, A, *tile, dtype=f32),
        vm(rows, width), vm(rows, width),
        vm(rows, hidden), vm(rows, hidden), vm(rows, hidden),
        vm(rows, hidden, dtype=f32), vm(rows, hidden, dtype=f32), vm(rows, hidden, dtype=f32),
        vm(S, C, T, B, A, *pair), vm(S, T, B, A, *pair), vm(S, T, B, A, *pair),
        vm(S, nq, A, *pair), vm(S, A, *pair), vm(S, na, *pair),
        vm(C, B, A, *tile, dtype=f32), vm(B, A, *tile, dtype=f32),
        vm(T * B, A, *tile, dtype=f32), vm(A, *tile, dtype=f32), vm(na, *tile, dtype=f32),
        pltpu.SemaphoreType.DMA((3,)),
        pltpu.SemaphoreType.DMA((count,)),
        pltpu.SemaphoreType.DMA((count,)),
    ]
    inside = pl.BlockSpec(memory_space=pltpu.VMEM)
    outside = pl.BlockSpec(memory_space=pl.ANY)
    shapes = (
        jax.ShapeDtypeStruct((group, feats), bf),
        jax.ShapeDtypeStruct((group, feats), bf),
        jax.ShapeDtypeStruct(expert_ids.shape, f32),
    )
    results = pl.pallas_call(
        functools.partial(kernel, A, B, T, count),
        out_shape=shapes,
        in_specs=[inside] * 4 + [outside] * 3,
        out_specs=(inside, inside, inside),
        scratch_shapes=scratch,
        compiler_params=pltpu.CompilerParams(
            collective_id=0, has_side_effects=True, vmem_limit_bytes=60 * 1024 * 1024
        ),
        cost_estimate=pl.CostEstimate(
            flops=12 * rows * width * hidden,
            bytes_accessed=6 * width * hidden,
            transcendentals=rows * hidden,
        ),
    )(tokens, out_grad, expert_ids, gate_probs, w_gate, w_up, w_down)
    return pl.pallas_call(
        settle, out_shape=shapes, in_specs=[inside] * 3, out_specs=(inside, inside, inside)
    )(*results)


def solution(mesh):
    placed = (
        P("expert", "tensor"),
        P("expert", "tensor"),
        P("expert", None),
        P("expert", None),
        P("expert", None, "tensor"),
        P("expert", None, "tensor"),
        P("expert", "tensor", None),
    )
    return jax.shard_map(
        per_device,
        mesh=mesh,
        in_specs=placed,
        out_specs=(P("expert", "tensor"), P("expert", "tensor"), P("expert", None)),
        check_vma=False,
    )
```

time: 46.5 us -> 39.2 us (0.84)
  local copies, waits for them, and re-layouts: 3.92 us -> 0 us
  Pallas kernels: 41.5 us -> 38.2 us
    unnamed x3 -> x0, local copies, waits for them, and re-layouts: 3.92 us -> none
    pallas_call x1 -> x2, Pallas kernels: 41.5 us -> 38.2 us  [the longest x1 36.9 us: per_device(): pl.pallas_call(functools.partial(kernel, A, B, T, count), out_shape=shape...]
where the time goes in v6:
time: 39.2 us; the launch traced here: 38.9 us
  Pallas kernels  38.2 us (97%)
  between operations  0.64 us (2%)
    pallas_call x1, Pallas kernels, per_device(): pl.pallas_call(functools.partial(kernel, A, B, T, count), out_shape=shape...  36.9 us
    pallas_call x1, Pallas kernels, per_device(): pl.pallas_call(settle, out_shape=shapes, in_specs=[inside] * 3, out_specs...  1.35 us

profile of v6, /device:TPU:0, one launch (start us, length us, event | category | flops | bytes accessed | tf_op | source)
XLA Modules:
  0.0 38.9 jit_solution(4485141786485028712)
XLA Ops:
  0.6 36.9 %shard_map.94 = (bf16[8,1024]{1,0:T(8,128)(2,1)}, bf16[8,1024]{1,0:T(8,128)(2,1)}, f32[8,8]{1,0:T(8,128)}) custom-call(bf16[8,1024]{1,0:T(8,128)(2,1)} %tok_ref.1, bf16[8,1024]{1,0:T(8,128)(2,1)} %grad_ref.1, s32[8,8]{1,0:T(8,128)} %ids_ref.1, f32[8,8]{1,0:T(8,128)} %prob_ref.1, bf16[1,2048,768]{2,1,0:T(8,128)(2,1)} %wg_hbm.1, bf16[1,2048,768]{2,1,0:T(8,128)(2,1)} %wu_hbm.1, ...), custom_call_target="tpu_custom_call" | custom-call | flops 2415919104 | bytes 9437184 | tf_op jit(solution)/shard_map/pallas_call | solution.py:340
  37.5 1.4 %shard_map.95 = (bf16[8,1024]{1,0:T(8,128)(2,1)}, bf16[8,1024]{1,0:T(8,128)(2,1)}, f32[8,8]{1,0:T(8,128)}) custom-call(bf16[8,1024]{1,0:T(8,128)(2,1)} %get-tuple-element.6.refs_0_, bf16[8,1024]{1,0:T(8,128)(2,1)} %get-tuple-element.7.refs_1_, f32[8,8]{1,0:T(8,128)} %get-tuple-element.8.refs_2_), custom_call_target="tpu_custom_call" | custom-call | tf_op jit(solution)/shard_map/pallas_call | solution.py:355

commit v7 on v6

--- a/solution.py
+++ b/solution.py
@@ -33,11 +33,11 @@
 
 def kernel(
     A, B, T, count,
-    tok_ref, grad_ref, ids_ref, prob_ref, wg_hbm, wu_hbm, wd_hbm,
+    tok_hbm, grad_hbm, ids_hbm, prob_hbm, wg_hbm, wu_hbm, wd_hbm,
     mixed_ref, tgrad_ref, pgrad_ref,
-    wg, wu, wd, g, pg, xs, og, hid, gga, gup, sum_gate, sum_up, sum_back,
+    tok_ref, grad_ref, ids_ref, prob_ref, wg, wu, wd, g, pg, xs, og, hid, gga, gup, sum_gate, sum_up, sum_back,
     parts, landed, sums, rq, v, rz, qr, qc, qx, qv, qz,
-    wsem, ssem, rsem,
+    isem, wsem, ssem, rsem,
 ):
     me = lax.axis_index("expert")
     t = lax.axis_index("tensor")
@@ -72,8 +72,19 @@
     peers = to_a + to_q + [to_c]
     for peer in peers:
         pl.semaphore_signal(barrier, inc=1, device_id=peer, device_id_type=MESH)
-    for load in loads:
+    small = [
+        pltpu.make_async_copy(src, dst, isem.at[i])
+        for i, (src, dst) in enumerate(
+            (
+                (tok_hbm, tok_ref), (grad_hbm, grad_ref),
+                (ids_hbm, ids_ref), (prob_hbm, prob_ref),
+            )
+        )
+    ]
+    for load in small + loads:
         load.start()
+    for load in small:
+        load.wait()
 
     ids = ids_ref[...]
     probs = prob_ref[...]
@@ -291,8 +302,15 @@
 
 
 def settle(*refs):
-    for source, target in zip(refs[: len(refs) // 2], refs[len(refs) // 2 :]):
-        target[...] = source[...]
+    *arrays, sem = refs
+    count = len(arrays) // 2
+    copies = [
+        pltpu.make_async_copy(arrays[i], arrays[count + i], sem.at[i]) for i in range(count)
+    ]
+    for copy in copies:
+        copy.start()
+    for copy in copies:
+        copy.wait()
 
 
 def per_device(tokens, out_grad, expert_ids, gate_probs, w_gate, w_up, w_down):
@@ -317,6 +335,8 @@
         return pltpu.VMEM(shape, dtype)
 
     scratch = [
+        vm(group, feats), vm(group, feats),
+        vm(*expert_ids.shape, dtype=jnp.int32), vm(*gate_probs.shape, dtype=f32),
         vm(width, hidden), vm(width, hidden), vm(hidden, width),
         vm(S, C, T * B, A, *pair), vm(C, B, A, *tile, dtype=f32),
         vm(rows, width), vm(rows, width),
@@ -326,6 +346,7 @@
         vm(S, nq, A, *pair), vm(S, A, *pair), vm(S, na, *pair),
         vm(C, B, A, *tile, dtype=f32), vm(B, A, *tile, dtype=f32),
         vm(T * B, A, *tile, dtype=f32), vm(A, *tile, dtype=f32), vm(na, *tile, dtype=f32),
+        pltpu.SemaphoreType.DMA((4,)),
         pltpu.SemaphoreType.DMA((3,)),
         pltpu.SemaphoreType.DMA((count,)),
         pltpu.SemaphoreType.DMA((count,)),
@@ -340,7 +361,7 @@
     results = pl.pallas_call(
         functools.partial(kernel, A, B, T, count),
         out_shape=shapes,
-        in_specs=[inside] * 4 + [outside] * 3,
+        in_specs=[outside] * 7,
         out_specs=(inside, inside, inside),
         scratch_shapes=scratch,
         compiler_params=pltpu.CompilerParams(
@@ -353,7 +374,11 @@
         ),
     )(tokens, out_grad, expert_ids, gate_probs, w_gate, w_up, w_down)
     return pl.pallas_call(
-        settle, out_shape=shapes, in_specs=[inside] * 3, out_specs=(inside, inside, inside)
+        settle,
+        out_shape=shapes,
+        in_specs=[outside] * 3,
+        out_specs=(outside, outside, outside),
+        scratch_shapes=[pltpu.SemaphoreType.DMA((3,))],
     )(*results)
 
 

time: 39.2 us -> 39.8 us (1.015)
  Pallas kernels: 38.2 us -> 38.9 us
    pallas_call x1, Pallas kernels: 1.35 us -> 2.25 us  [per_device(): pl.pallas_call(settle, out_shape=shapes, in_specs=[outside] * 3, out_spec...]
where the time goes in v7:
time: 39.8 us; the launch traced here: 39.6 us
  Pallas kernels  38.9 us (98%)
  between operations  0.64 us (2%)
    pallas_call x1, Pallas kernels, per_device(): pl.pallas_call(functools.partial(kernel, A, B, T, count), out_shape=shape...  36.7 us
    pallas_call x1, Pallas kernels, per_device(): pl.pallas_call(settle, out_shape=shapes, in_specs=[outside] * 3, out_spec...  2.25 us

profile of v7, /device:TPU:0, one launch (start us, length us, event | category | flops | bytes accessed | tf_op | source)
XLA Modules:
  0.0 39.6 jit_solution(8729203334461209247)
XLA Ops:
  0.6 36.7 %shard_map.94 = (bf16[8,1024]{1,0:T(8,128)(2,1)}, bf16[8,1024]{1,0:T(8,128)(2,1)}, f32[8,8]{1,0:T(8,128)}) custom-call(bf16[8,1024]{1,0:T(8,128)(2,1)} %tok_hbm.1, bf16[8,1024]{1,0:T(8,128)(2,1)} %grad_hbm.1, s32[8,8]{1,0:T(8,128)} %ids_hbm.1, f32[8,8]{1,0:T(8,128)} %prob_hbm.1, bf16[1,2048,768]{2,1,0:T(8,128)(2,1)} %wg_hbm.1, bf16[1,2048,768]{2,1,0:T(8,128)(2,1)} %wu_hbm.1, ...), custom_call_target="tpu_custom_call" | custom-call | flops 2415919104 | bytes 9437184 | tf_op jit(solution)/shard_map/pallas_call | solution.py:361
  37.3 2.2 %shard_map.95 = (bf16[8,1024]{1,0:T(8,128)(2,1)}, bf16[8,1024]{1,0:T(8,128)(2,1)}, f32[8,8]{1,0:T(8,128)}) custom-call(bf16[8,1024]{1,0:T(8,128)(2,1)} %get-tuple-element.6.refs_0_, bf16[8,1024]{1,0:T(8,128)(2,1)} %get-tuple-element.7.refs_1_, f32[8,8]{1,0:T(8,128)} %get-tuple-element.8.refs_2_), custom_call_target="tpu_custom_call" | custom-call | tf_op jit(solution)/shard_map/pallas_call | solution.py:376

commit v8 on v7

--- a/solution.py
+++ b/solution.py
@@ -57,7 +57,7 @@
         return lax.rem(value + r, size)
 
     q = t * B + b
-    offsets = [(i, j) for i in range(T) for j in range(B) if i or j]
+    offsets = [(i, j) for i in range(T) for j in range(B) if i or j][::-1]
     to_a = [spot(turn(a, r, A), b, c, t) for r in range(1, A)]
     to_b = [spot(a, turn(b, r, B), c, t) for r in range(1, B)]
     to_q = [spot(a, turn(b, j, B), c, turn(t, i, T)) for i, j in offsets]
@@ -302,15 +302,8 @@
 
 
 def settle(*refs):
-    *arrays, sem = refs
-    count = len(arrays) // 2
-    copies = [
-        pltpu.make_async_copy(arrays[i], arrays[count + i], sem.at[i]) for i in range(count)
-    ]
-    for copy in copies:
-        copy.start()
-    for copy in copies:
-        copy.wait()
+    for source, target in zip(refs[: len(refs) // 2], refs[len(refs) // 2 :]):
+        target[...] = source[...]
 
 
 def per_device(tokens, out_grad, expert_ids, gate_probs, w_gate, w_up, w_down):
@@ -374,11 +367,7 @@
         ),
     )(tokens, out_grad, expert_ids, gate_probs, w_gate, w_up, w_down)
     return pl.pallas_call(
-        settle,
-        out_shape=shapes,
-        in_specs=[outside] * 3,
-        out_specs=(outside, outside, outside),
-        scratch_shapes=[pltpu.SemaphoreType.DMA((3,))],
+        settle, out_shape=shapes, in_specs=[inside] * 3, out_specs=(inside, inside, inside)
     )(*results)
 
 

time: 39.8 us -> 38.6 us (0.970)
  Pallas kernels: 38.9 us -> 37.6 us
    pallas_call x1, Pallas kernels: 2.25 us -> 1.35 us  [per_device(): pl.pallas_call(settle, out_shape=shapes, in_specs=[inside] * 3, out_specs...]
    pallas_call x1, Pallas kernels: 36.7 us -> 36.3 us  [per_device(): pl.pallas_call(functools.partial(kernel, A, B, T, count), out_shape=shape...]
where the time goes in v8:
time: 38.6 us; the launch traced here: 38.2 us
  Pallas kernels  37.6 us (97%)
  between operations  0.64 us (2%)
    pallas_call x1, Pallas kernels, per_device(): pl.pallas_call(functools.partial(kernel, A, B, T, count), out_shape=shape...  36.3 us
    pallas_call x1, Pallas kernels, per_device(): pl.pallas_call(settle, out_shape=shapes, in_specs=[inside] * 3, out_specs...  1.35 us

profile of v8, /device:TPU:0, one launch (start us, length us, event | category | flops | bytes accessed | tf_op | source)
XLA Modules:
  0.0 38.2 jit_solution(17623298085420084154)
XLA Ops:
  0.6 36.3 %shard_map.94 = (bf16[8,1024]{1,0:T(8,128)(2,1)}, bf16[8,1024]{1,0:T(8,128)(2,1)}, f32[8,8]{1,0:T(8,128)}) custom-call(bf16[8,1024]{1,0:T(8,128)(2,1)} %tok_hbm.1, bf16[8,1024]{1,0:T(8,128)(2,1)} %grad_hbm.1, s32[8,8]{1,0:T(8,128)} %ids_hbm.1, f32[8,8]{1,0:T(8,128)} %prob_hbm.1, bf16[1,2048,768]{2,1,0:T(8,128)(2,1)} %wg_hbm.1, bf16[1,2048,768]{2,1,0:T(8,128)(2,1)} %wu_hbm.1, ...), custom_call_target="tpu_custom_call" | custom-call | flops 2415919104 | bytes 9437184 | tf_op jit(solution)/shard_map/pallas_call | solution.py:354
  36.9 1.4 %shard_map.95 = (bf16[8,1024]{1,0:T(8,128)(2,1)}, bf16[8,1024]{1,0:T(8,128)(2,1)}, f32[8,8]{1,0:T(8,128)}) custom-call(bf16[8,1024]{1,0:T(8,128)(2,1)} %get-tuple-element.6.refs_0_, bf16[8,1024]{1,0:T(8,128)(2,1)} %get-tuple-element.7.refs_1_, f32[8,8]{1,0:T(8,128)} %get-tuple-element.8.refs_2_), custom_call_target="tpu_custom_call" | custom-call | tf_op jit(solution)/shard_map/pallas_call | solution.py:369
